TPU v7x, 128 devices: a whole 4x4x4 slice. The times are simulated.
128 devices in a mesh: row: 8 (over y, z_hi), col: 16 (over x, z_lo, core).
Axes of the slice: x: 4, y: 4, z: 4 (z_hi: 2, z_lo: 2; z = z_hi * 2 + z_lo), core: 2. Of those that a mesh axis runs over, the one named last changes fastest.
Arguments:
- source_table: bfloat16 [8, 2048, 400], P('row', 'col'), may hold values from -3 to 3
- dest_table: bfloat16 [16, 2048, 400], P('col', 'row'), may hold values from -3 to 3
- relations: float32 [1345, 400], replicated, may hold values from -4 to 4
- rel_history: float32 [1345, 400], replicated, may hold values from 0.5 to 5
- src_ids: int32 [8, 16, 2, 4000], P('row', 'col'), may hold values from 0 to 2047
- rel_ids: int32 [8, 16, 2, 4000], P('row', 'col'), may hold values from 0 to 1344
- dst_ids: int32 [8, 16, 2, 4000], P('row', 'col'), may hold values from 0 to 2047
- neg_ids: int32 [8, 16, 2, 4, 1000], P('row', 'col'), may hold values from 0 to 2047
- counts: int32 [8, 16, 2], P('row', 'col'), may hold values from 500 to 4000, as said below
Outputs:
- source_out: bfloat16 [8, 2048, 400], P('row', 'col')
- dest_out: bfloat16 [16, 2048, 400], P('col', 'row')
- relations_out: float32 [1345, 400], replicated
- history_out: float32 [1345, 400], replicated
Inputs may be any that keep to these rules, and one draw needn't show every extreme that they name: `counts`: live edges come first in each list; some bucket holds 4000 live edges in every draw.
All inputs are finite; a program needn't handle non-finite values.
Results may differ from a plain program's by a relative error of at most 0.029.
Values may be sent and summed in bfloat16 or wider, within the bound.
A program may use at most 128 MiB of HBM per device.

v0:
```python
import jax
import jax.numpy as jnp
from jax import lax
from jax.sharding import PartitionSpec as P

entity_rate = 0.3
relation_rate = 0.5


def swapped(shard, axis, bit):
    return lax.ppermute(shard, axis, [(i, i ^ 1 << bit) for i in range(lax.axis_size(axis))])


def block_terms(
    position,
    totals,
    src_block,
    dst_block,
    relations,
    src_rows,
    rel_rows,
    dst_rows,
    neg_table,
    live_edges,
):
    grad_src, grad_dst, grad_rel = totals
    position = jnp.asarray(position).astype(jnp.int32)
    edges_per = src_rows.shape[0] // neg_table.shape[0]
    negs_per = neg_table.shape[1]
    offset = position * edges_per
    src_pick = lax.dynamic_slice_in_dim(src_rows, offset, edges_per)
    rel_pick = lax.dynamic_slice_in_dim(rel_rows, offset, edges_per)
    dst_pick = lax.dynamic_slice_in_dim(dst_rows, offset, edges_per)
    neg_pick = lax.dynamic_index_in_dim(neg_table, position, 0, keepdims=False)
    alive = (offset + jnp.arange(edges_per, dtype=jnp.int32) < live_edges).astype(jnp.float32)
    source = src_block[src_pick].astype(jnp.float32)
    relation = relations[rel_pick]
    target = dst_block[dst_pick].astype(jnp.float32)
    negatives = dst_block[neg_pick]
    half_width = source.shape[1] // 2
    src_re, src_im = (source[:, :half_width], source[:, half_width:])
    rel_re, rel_im = (relation[:, :half_width], relation[:, half_width:])
    rotated = jnp.concatenate(
        [src_re * rel_re - src_im * rel_im, src_re * rel_im + src_im * rel_re], axis=1
    )
    rotated_b = rotated.astype(jnp.bfloat16)
    pos_score = jnp.sum(rotated * target, axis=1)
    neg_score = lax.dot_general(
        rotated_b, negatives, (((1,), (1,)), ((), ())), preferred_element_type=jnp.float32
    )
    grad_pos = -alive * jax.nn.sigmoid(-pos_score)
    grad_neg = (jax.nn.sigmoid(neg_score) * (alive[:, None] / negs_per)).astype(jnp.bfloat16)
    grad_rot = grad_pos[:, None] * target + jnp.dot(
        grad_neg, negatives, preferred_element_type=jnp.float32
    )
    grad_re, grad_im = (grad_rot[:, :half_width], grad_rot[:, half_width:])
    grad_source = jnp.concatenate(
        [grad_re * rel_re + grad_im * rel_im, grad_im * rel_re - grad_re * rel_im], axis=1
    )
    grad_relation = jnp.concatenate(
        [grad_re * src_re + grad_im * src_im, grad_im * src_re - grad_re * src_im], axis=1
    )
    grad_negrows = lax.dot_general(
        grad_neg, rotated_b, (((0,), (0,)), ((), ())), preferred_element_type=jnp.float32
    )
    grad_src = grad_src.at[src_pick].add(grad_source)
    grad_dst = grad_dst.at[dst_pick].add(grad_pos[:, None] * rotated)
    grad_dst = grad_dst.at[neg_pick].add(grad_negrows)
    grad_rel = grad_rel.at[rel_pick].add(grad_relation)
    return (grad_src, grad_dst, grad_rel)


def bucket_grads(
    src_block, dst_block, relations, src_rows, rel_rows, dst_rows, neg_table, live_edges
):
    empty = (
        jnp.zeros(src_block.shape, jnp.float32),
        jnp.zeros(dst_block.shape, jnp.float32),
        jnp.zeros(relations.shape, jnp.float32),
    )
    edges_per = src_rows.shape[0] // neg_table.shape[0]
    busy = (live_edges + edges_per - 1) // edges_per

    def advance(position, totals):
        return block_terms(
            position,
            totals,
            src_block,
            dst_block,
            relations,
            src_rows,
            rel_rows,
            dst_rows,
            neg_table,
            live_edges,
        )

    return lax.fori_loop(0, busy, advance, empty)


def relation_step(relations, history, grads):
    total = lax.psum(grads, ("row", "col"))
    history = history + total * total
    return (relations - relation_rate * total / jnp.sqrt(history), history)


def apply_step(table, grads):
    return (table.astype(jnp.float32) - entity_rate * grads).astype(jnp.bfloat16)


def on_device(
    source_table, dest_table, relations, rel_history, src_ids, rel_ids, dst_ids, neg_ids, counts
):
    partner_bit = (lax.axis_size("col") // 2).bit_length() - 1
    src_slice = source_table[0]
    dst_slice = dest_table[0]
    src_block = lax.all_gather(src_slice, "col", axis=0, tiled=True)
    dst_block = lax.all_gather(dst_slice, "row", axis=0, tiled=True)
    grad_src, grad_dst, grad_rel = bucket_grads(
        src_block,
        dst_block,
        relations,
        src_ids[0, 0, 0],
        rel_ids[0, 0, 0],
        dst_ids[0, 0, 0],
        neg_ids[0, 0, 0],
        counts[0, 0, 0],
    )
    relations_mid, history_mid = relation_step(relations, rel_history, grad_rel)
    src_part = lax.psum_scatter(
        grad_src.astype(jnp.bfloat16), "col", scatter_dimension=0, tiled=True
    ).astype(jnp.float32)
    src_share = apply_step(src_slice, src_part)
    src_next = lax.all_gather(src_share, "col", axis=0, tiled=True)
    dst_part = lax.psum_scatter(
        grad_dst.astype(jnp.bfloat16), "row", scatter_dimension=0, tiled=True
    ).astype(jnp.float32)
    dst_share = apply_step(dst_slice, dst_part)
    partner_share = swapped(dst_share, "col", partner_bit)
    partner_block = lax.all_gather(partner_share, "row", axis=0, tiled=True)
    grad_src2, grad_dst2, grad_rel2 = bucket_grads(
        src_next,
        partner_block,
        relations_mid,
        src_ids[0, 0, 1],
        rel_ids[0, 0, 1],
        dst_ids[0, 0, 1],
        neg_ids[0, 0, 1],
        counts[0, 0, 1],
    )
    relations_end, history_end = relation_step(relations_mid, history_mid, grad_rel2)
    src_final = lax.psum_scatter(
        grad_src2.astype(jnp.bfloat16), "col", scatter_dimension=0, tiled=True
    ).astype(jnp.float32)
    source_out = apply_step(src_share, src_final)
    moved = swapped(grad_dst2.astype(jnp.bfloat16), "col", partner_bit)
    owned_grads = lax.psum_scatter(
        moved.astype(jnp.float32).astype(jnp.bfloat16), "row", scatter_dimension=0, tiled=True
    ).astype(jnp.float32)
    dest_out = apply_step(dst_share, owned_grads)
    return (source_out[None], dest_out[None], relations_end, history_end)


def solution(mesh):
    placed = (
        P("row", "col", None),
        P("col", "row", None),
        P(),
        P(),
        P("row", "col", None, None),
        P("row", "col", None, None),
        P("row", "col", None, None),
        P("row", "col", None, None, None),
        P("row", "col", None),
    )
    return jax.shard_map(
        on_device,
        mesh=mesh,
        in_specs=placed,
        out_specs=(P("row", "col", None), P("col", "row", None), P(), P()),
        check_vma=False,
    )
```

profile of v0, /device:TPU:25, one launch (start us, length us, event | category | flops | bytes accessed | tf_op | source)
XLA Modules:
  0.0 1726.4 jit_solution(200815875541459834)
XLA Ops:
  18.7 47.2 %all-gather.13.cloned.1.call-done = bf16[1,2048,400]{2,1,0:T(8,128)(2,1)} async-done(((bf16[1,256,400]{2,1,0:T(8,128)(2,1)}), bf16[1,2048,400]{2,1,0:T(8,128)(2,1)}) %all-gather.13.cloned.1.call-update) | async-done | bytes 1638416 | tf_op jit(solution)/shard_map/all_gather | solution.py:118
  65.9 37.6 %all-gather.11.cloned.1.call-done = bf16[1,2048,400]{2,1,0:T(8,128)(2,1)} async-done(((bf16[1,128,400]{2,1,0:T(8,128)(2,1)}), bf16[1,2048,400]{2,1,0:T(8,128)(2,1)}) %all-gather.11.cloned.1.call-update) | async-done | bytes 1638416 | tf_op jit(solution)/shard_map/all_gather | solution.py:117
  110.8 222.8 %while.28 = (s32[]{:T(128)}, f32[2048,400]{1,0:T(8,128)}, f32[2048,400]{1,0:T(8,128)}, f32[1345,400]{1,0:T(8,128)}, s32[]{:T(128)}, /*index=5*/s32[4000]{0:T(102...) while((s32[]{:T(128)}, f32[2048,400]{1,0:T(8,128)}, ...), condition=%wide.region_6.7_spmd, body=%wide.region_0.6_spmd.sunk | while | flops 2418224640 | bytes 134924992 | solution.py:98
  110.9 7.0 gather_fusion.2
  124.7 6.0 gather_fusion.3
  135.2 5.1 gather_fusion
  144.8 5.1 gather_fusion.1
  150.6 3.6 multiply_convert_fusion.4
  163.3 10.6 scatter_fusion.3
  173.9 4.4 fusion.73
  182.5 11.4 scatter_fusion.1
  194.0 11.5 scatter_fusion.2
  210.7 11.3 scatter_fusion
  222.1 7.0 gather_fusion.2
  236.0 6.0 gather_fusion.3
  246.4 5.1 gather_fusion
  256.0 5.1 gather_fusion.1
  261.8 3.5 multiply_convert_fusion.4
  274.6 10.6 scatter_fusion.3
  285.2 4.4 fusion.73
  293.8 11.4 scatter_fusion.1
  305.2 11.5 scatter_fusion.2
  321.9 11.3 scatter_fusion
  339.4 4.5 copy.82
  346.2 275.0 %reduce-scatter.13.cloned.1.call-done = bf16[128,400]{1,0:T(8,128)(2,1)} async-done(((bf16[2048,400]{1,0:T(8,128)(2,1)}), bf16[128,400]{1,0:T(8,128)(2,1)}) %reduce-scatter.13.cloned.1.call-update) | async-done | bytes 102416
  623.0 73.1 %reduce-scatter.9.cloned.1.call-done = bf16[256,400]{0,1:T(8,128)(2,1)} async-done(((bf16[2048,400]{0,1:T(8,128)(2,1)}), bf16[256,400]{0,1:T(8,128)(2,1)}) %reduce-scatter.9.cloned.1.call-update) | async-done | bytes 204816 | tf_op jit(solution)/shard_map/reduce_scatter | solution.py:135
  705.4 147.0 %all-reduce.3.cloned.1.call-done = f32[1345,400]{0,1:T(8,128)} async-done(((f32[1345,400]{0,1:T(8,128)}), f32[1345,400]{0,1:T(8,128)}) %all-reduce.3.cloned.1.call-update) | async-done | bytes 2152016 | tf_op jit(solution)/shard_map/psum | solution.py:102
  858.2 31.5 %all-gather.7.cloned.1.call-done = bf16[2048,400]{0,1:T(8,128)(2,1)} async-done(((bf16[128,400]{0,1:T(8,128)(2,1)}), bf16[2048,400]{0,1:T(8,128)(2,1)}) %all-gather.7.cloned.1.call-update) | async-done | bytes 1638416 | tf_op jit(solution)/shard_map/all_gather | solution.py:134
  889.7 3.7 copy.83
  893.4 50.5 %all-gather.9.cloned.1.call-done = bf16[2048,400]{0,1:T(8,128)(2,1)} async-done(((bf16[256,400]{0,1:T(8,128)(2,1)}), bf16[2048,400]{0,1:T(8,128)(2,1)}) %all-gather.9.cloned.1.call-update) | async-done | bytes 1638416 | tf_op jit(solution)/shard_map/all_gather | solution.py:140
  953.7 113.9 %while.29 = (s32[]{:T(128)}, f32[2048,400]{1,0:T(8,128)}, f32[2048,400]{1,0:T(8,128)}, f32[1345,400]{1,0:T(8,128)}, s32[]{:T(128)}, /*index=5*/s32[4000]{0:T(102...) while((s32[]{:T(128)}, f32[2048,400]{1,0:T(8,128)}, ...), condition=%wide.region_16.17_spmd, body=%wide.region_10.16_spmd.sunk | while | flops 2418224640 | bytes 134924992 | solution.py:98
  954.7 7.1 gather_fusion.6
  969.3 6.0 gather_fusion.7
  979.9 5.1 gather_fusion.4
  990.2 5.0 gather_fusion.5
  995.9 3.6 multiply_convert_fusion.5
  1008.7 10.6 scatter_fusion.7
  1019.3 4.4 fusion.85
  1027.9 11.4 scatter_fusion.5
  1039.4 11.5 scatter_fusion.6
  1056.2 11.3 scatter_fusion.4
  1076.9 4.5 copy.87
  1081.4 229.9 %collective-permute-start.1 = (bf16[2048,400]{0,1:T(8,128)(2,1)}, bf16[2048,400]{0,1:T(8,128)(2,1)}, u32[]{:S(2)}, u32[]{:S(2)}) collective-permute-start(bf16[2048,400]{0,1:T(8,128)(2,1)} %copy.87), channel_id=1, source_target_pairs={{0,8},{1,9},{2,10},{3,11},{4,12},{5,13},{6,14},{7,15},{8,0},{9,1},... | collective-permute-start | bytes 4915208 | tf_op jit(solution)/shard_map/ppermute | solution.py:11
  1311.2 34.0 %collective-permute-done.1 = bf16[2048,400]{0,1:T(8,128)(2,1)} collective-permute-done((bf16[2048,400]{0,1:T(8,128)(2,1)}, bf16[2048,400]{0,1:T(8,128)(2,1)}, u32[]{:S(2)}, u32[]{:S(2)}) %collective-permute-start.1) | collective-permute-done | bytes 1638432 | tf_op jit(solution)/shard_map/ppermute | solution.py:11
  1345.2 235.4 %all-reduce.5.cloned.1.call-done = f32[1345,400]{0,1:T(8,128)} async-done(((f32[1345,400]{0,1:T(8,128)}), f32[1345,400]{0,1:T(8,128)}) %all-reduce.5.cloned.1.call-update) | async-done | bytes 2152016 | tf_op jit(solution)/shard_map/psum | solution.py:102
  1580.6 5.7 multiply_subtract_fusion.6
  1586.3 56.0 %reduce-scatter.15.cloned.1.call-done = bf16[128,400]{1,0:T(8,128)(2,1)} async-done(((bf16[2048,400]{1,0:T(8,128)(2,1)}), bf16[128,400]{1,0:T(8,128)(2,1)}) %reduce-scatter.15.cloned.1.call-update) | async-done | bytes 102416
  1644.0 73.5 %reduce-scatter.11.cloned.1.call-done = bf16[256,400]{0,1:T(8,128)(2,1)} async-done(((bf16[2048,400]{0,1:T(8,128)(2,1)}), bf16[256,400]{0,1:T(8,128)(2,1)}) %reduce-scatter.11.cloned.1.call-update) | async-done | bytes 204816 | tf_op jit(solution)/shard_map/reduce_scatter | solution.py:157
  (220 shorter events, 172.1 us)
Async XLA Ops:
  7.2 58.7 %all-gather.13.cloned.1.call-start = ((), (), s32[]{:S(2)}) async-start(), calls=%async_computation.11 | async-start | bytes 2359296 | tf_op jit(solution)/shard_map/all_gather | solution.py:118
  9.0 94.5 %all-gather.11.cloned.1.call-start = ((), (), s32[]{:S(2)}) async-start(), calls=%async_computation.10 | async-start | bytes 2228224 | tf_op jit(solution)/shard_map/all_gather | solution.py:117
  10.7 610.5 %reduce-scatter.13.cloned.1.call-start = ((), (), s32[]{:S(2)}) async-start(), calls=%async_computation.12 | async-start | bytes 2228224
  12.8 3.4 copy-start.30
  12.8 4.0 copy-start.31
  12.8 4.6 copy-start.32
  12.8 5.2 copy-start.33
  108.5 2.3 copy-start
  132.1 1.4 copy-start.8
  132.1 1.6 copy-start.12
  150.5 4.9 copy-start.16
  150.5 4.9 copy-start.20
  155.4 1.6 copy-start.9
  155.4 1.9 copy-start.13
  173.9 4.4 copy-start.6
  194.0 11.5 copy-start.18
  243.3 1.4 copy-start.8
  243.3 1.6 copy-start.12
  261.8 4.9 copy-start.16
  261.8 4.9 copy-start.20
  266.7 1.6 copy-start.9
  266.7 1.9 copy-start.13
  285.2 4.4 copy-start.6
  305.2 11.5 copy-start.18
  339.4 356.8 %reduce-scatter.9.cloned.1.call-start = ((), (), s32[]{:S(2)}) async-start(), calls=%async_computation.6 | async-start | bytes 1843200 | tf_op jit(solution)/shard_map/reduce_scatter | solution.py:135
  339.4 4.6 copy-start.1
  344.0 508.4 %all-reduce.3.cloned.1.call-start = ((), (), s32[]{:S(2)}) async-start(), calls=%async_computation.5 | async-start | bytes 4505600 | tf_op jit(solution)/shard_map/psum | solution.py:102
  346.1 276.1 %copy-start.28 = (bf16[1,128,400]{1,2,0:T(8,128)(2,1)S(1)}, bf16[1,128,400]{1,2,0:T(8,128)(2,1)}, u32[]{:S(2)}) copy-start(bf16[1,128,400]{1,2,0:T(8,128)(2,1)} %param.13) | copy-start | bytes 307204
  346.1 350.0 %copy-start.25 = (bf16[1,256,400]{1,2,0:T(8,128)(2,1)S(1)}, bf16[1,256,400]{1,2,0:T(8,128)(2,1)}, u32[]{:S(2)}) copy-start(bf16[1,256,400]{1,2,0:T(8,128)(2,1)} %param.14) | copy-start | bytes 614404
  346.2 543.5 %all-gather.7.cloned.1.call-start = ((), (), s32[]{:S(2)}) async-start(), calls=%async_computation.4 | async-start | bytes 1740800 | tf_op jit(solution)/shard_map/all_gather | solution.py:134
  623.0 321.0 %all-gather.9.cloned.1.call-start = ((), (), s32[]{:S(2)}) async-start(), calls=%async_computation.7 | async-start | bytes 1843200 | tf_op jit(solution)/shard_map/all_gather | solution.py:140
  697.8 6.1 collective-permute-start
  704.7 876.0 %all-reduce.5.cloned.1.call-start = ((), (), s32[]{:S(2)}) async-start(), calls=%async_computation.9 | async-start | bytes 4505600 | tf_op jit(solution)/shard_map/psum | solution.py:102
  855.8 2.4 copy-start.22
  976.7 1.6 copy-start.14
  978.4 1.5 copy-start.4
  995.9 4.9 copy-start.17
  995.9 4.9 copy-start.21
  1000.8 1.6 copy-start.11
  1000.8 1.9 copy-start.15
  1019.3 4.4 copy-start.7
  1039.4 11.5 copy-start.19
  1071.0 571.3 %reduce-scatter.15.cloned.1.call-start = ((), (), s32[]{:S(2)}) async-start(), calls=%async_computation.13 | async-start | bytes 2228224
  1076.8 640.7 %reduce-scatter.11.cloned.1.call-start = ((), (), s32[]{:S(2)}) async-start(), calls=%async_computation.8 | async-start | bytes 1843200 | tf_op jit(solution)/shard_map/reduce_scatter | solution.py:157
  1076.8 503.8 %copy-start.23 = (f32[1345,400]{0,1:T(8,128)S(1)}, f32[1345,400]{0,1:T(8,128)}, u32[]{:S(2)}) copy-start(f32[1345,400]{0,1:T(8,128)} %copy-done.22) | copy-start | bytes 6456004
  1081.4 263.8 %collective-permute-start.1 = (bf16[2048,400]{0,1:T(8,128)(2,1)}, bf16[2048,400]{0,1:T(8,128)(2,1)}, u32[]{:S(2)}, u32[]{:S(2)}) collective-permute-start(bf16[2048,400]{0,1:T(8,128)(2,1)} %copy.87), channel_id=1, source_target_pairs={{0,8},{1,9},{2,10},{3,11},{4,12},{5,13},{6,14},{7,15},{8,0},{9,1},... | collective-permute-start | bytes 4915208 | tf_op jit(solution)/shard_map/ppermute | solution.py:11
  1345.2 298.1 %copy-start.24 = (bf16[128,400]{0,1:T(8,128)(2,1)S(1)}, bf16[128,400]{0,1:T(8,128)(2,1)}, u32[]{:S(2)}) copy-start(bf16[128,400]{0,1:T(8,128)(2,1)} %fusion.22) | copy-start | bytes 307204
  1345.2 372.3 %copy-start.27 = (bf16[256,400]{0,1:T(8,128)(2,1)S(1)}, bf16[256,400]{0,1:T(8,128)(2,1)}, u32[]{:S(2)}) copy-start(bf16[256,400]{0,1:T(8,128)(2,1)} %copy-done.26) | copy-start | bytes 614404
  (11 other events, 13.9 us)
Sparse Core Ops, SparseCore 0:
  10.9 54.9 all-gather.12
  68.1 35.2 all-gather.10
  339.5 281.7 reduce-scatter.12
  624.8 71.3 reduce-scatter.8
  701.4 150.9 all-reduce.2
  854.5 35.1 all-gather.6
  892.7 51.2 all-gather.8
  1071.1 509.4 all-reduce.4
  1583.0 59.2 reduce-scatter.14
  1645.8 71.6 reduce-scatter.10
where the time goes:
time: 1740 us; the launch traced here: 1730 us
  waiting for transfers between devices  1060 us (61%)
  starting transfers between devices  233 us (13%)
  local copies, waits for them, and re-layouts  196 us (11%)
  other arithmetic  189 us (11%)
  matrix products  27.2 us (2%)
    psum x2, waiting for transfers between devices, relation_step(): total = lax.psum(grads, ('row', 'col'))  382 us
    unnamed x12, waiting for transfers between devices  331 us
    ppermute x2, starting transfers between devices, swapped(): lax.ppermute(shard, axis, [(i, i ^ 1 << bit) for i in range(lax.axis_size...  233 us
    reduce_scatter x1, waiting for transfers between devices, on_device(): lax.psum_scatter(moved.astype(jnp.float32).astype(jnp.bfloat16), 'row', s...  73.5 us
    reduce_scatter x1, waiting for transfers between devices, on_device(): lax.psum_scatter(grad_dst.astype(jnp.bfloat16), 'row', scatter_dimension=...  73.1 us
    all_gather x1, waiting for transfers between devices, on_device(): partner_block = lax.all_gather(partner_share, 'row', axis=0, tiled=True)  50.5 us
    all_gather x1, waiting for transfers between devices, on_device(): dst_block = lax.all_gather(dst_slice, 'row', axis=0, tiled=True)  47.2 us
    all_gather x1, waiting for transfers between devices, on_device(): src_block = lax.all_gather(src_slice, 'col', axis=0, tiled=True)  37.6 us
  transfers between devices with their start and end apart: 12, of which 12 were waited for; matrix products, arithmetic and copies ran while one was open for 3% of the time, Pallas kernels for 0%

commit v1 on v0

v1 whole, which is shorter than its diff:
```python
import functools
import jax
import jax.numpy as jnp
from jax import lax
from jax.experimental import pallas as pl
from jax.experimental.pallas import tpu as pltpu
from jax.sharding import PartitionSpec as P

F32, BF16 = jnp.float32, jnp.bfloat16
MESH = pl.DeviceIdType.MESH
NT = (((1,), (1,)), ((), ()))
entity_rate = 0.3
relation_rate = 0.5
N_ROW, N_COL = 8, 16
HALF_COL = 8
TILE, LIVE = 512, 500
TILES = 8
CHUNK = 256
REL_CUT = 96
REL_ROWS = REL_CUT * N_COL
VMEM_BYTES = 60 * 2**20


def onehot(rows, base, ids):
    at = lax.broadcasted_iota(jnp.int32, (rows, ids.shape[1]), 0) + base
    return jnp.where(at == ids, 1.0, 0.0).astype(BF16)


def bucket_kernel(
    pack_ref, src_ref, dst_ref, rel_ref, gs_out, gd_out, gr_out,
    acc_s, acc_d, acc_r, ohs, ohr, mm, cnt, dnat, relt,
):
    width, rows = src_ref.shape
    half = width // 2
    rels = rel_ref.shape[0]
    wide = relt.shape[1]
    blocks = TILES // 2
    acc_s[...] = jnp.zeros_like(acc_s)
    acc_d[...] = jnp.zeros_like(acc_d)
    acc_r[...] = jnp.zeros_like(acc_r)
    relt[...] = jnp.zeros_like(relt)
    eye = onehot(CHUNK, 0, lax.broadcasted_iota(jnp.int32, (1, CHUNK), 1))
    for c in range(rows // CHUNK):
        cut = pl.ds(c * CHUNK, CHUNK)
        turned = lax.dot_general(eye, dst_ref[:, cut], NT, preferred_element_type=F32)
        dnat[cut, :] = turned.astype(BF16)
    eye = onehot(width, 0, lax.broadcasted_iota(jnp.int32, (1, width), 1))
    for start in range(0, rels, CHUNK):
        cut = pl.ds(start, min(CHUNK, rels - start))
        turned = lax.dot_general(eye, rel_ref[cut, :].astype(BF16), NT, preferred_element_type=F32)
        relt[:, cut] = turned.astype(BF16)
    for k in range(blocks):
        total = 0.0
        for h in range(2):
            ids = pack_ref[pl.ds(3 * TILES + 2 * k + h, 1), :]
            low = onehot(128, 0, jnp.where(ids < 0, -1, ids & 127))
            high = onehot(rows // 128, 0, jnp.where(ids < 0, -1, ids >> 7))
            total = total + lax.dot_general(low, high, NT, preferred_element_type=F32)
        cnt[k] = total * (1.0 / (2 * LIVE))

    def tile(t, _):
        sid = pack_ref[pl.ds(t, 1), :]
        rid = pack_ref[pl.ds(TILES + t, 1), :]
        did = pack_ref[pl.ds(2 * TILES + t, 1), :]
        for c in range(rows // CHUNK):
            ohs[pl.ds(c * CHUNK, CHUNK), :] = onehot(CHUNK, c * CHUNK, sid)
        ohr[...] = onehot(wide, 0, rid)
        alive = jnp.where(did >= 0, 0.5, 0.0)
        s = jnp.dot(src_ref[...], ohs[...], preferred_element_type=F32)
        r = jnp.dot(relt[...], ohr[...], preferred_element_type=F32)
        sre, sim, rre, rim = s[:half], s[half:], r[:half], r[half:]
        rot = jnp.concatenate([sre * rre - sim * rim, sre * rim + sim * rre], 0)
        rot = (rot * alive).astype(BF16)
        weight = cnt[t // 2]
        for c in range(rows // CHUNK):
            cut = pl.ds(c * CHUNK, CHUNK)
            lean = jnp.tanh(jnp.dot(dnat[cut, :], rot, preferred_element_type=F32))
            share = jnp.concatenate([weight[:, 2 * c : 2 * c + 1], weight[:, 2 * c + 1 : 2 * c + 2]], 0)
            hit = lax.broadcasted_iota(jnp.int32, (CHUNK, TILE), 0) + c * CHUNK == did
            slope = jnp.where(hit, share + 1, share)
            mm[cut, :] = (slope * lean + jnp.where(hit, share - 1, share)).astype(BF16)
        g = jnp.dot(dst_ref[...], mm[...], preferred_element_type=F32) * alive
        acc_d[...] += lax.dot_general(rot, mm[...], NT, preferred_element_type=F32)
        gre, gim = g[:half], g[half:]
        gs = jnp.concatenate([gre * rre + gim * rim, gim * rre - gre * rim], 0).astype(BF16)
        gr = jnp.concatenate([gre * sre + gim * sim, gim * sre - gre * sim], 0).astype(BF16)
        acc_s[...] += lax.dot_general(gs, ohs[...], NT, preferred_element_type=F32)
        acc_r[pl.ds(0, wide), :] += lax.dot_general(ohr[...], gr, NT, preferred_element_type=F32)
        return 0

    lax.fori_loop(0, jnp.max(pack_ref[pl.ds(4 * TILES, TILES), :]), tile, 0)
    gs_out[...] = acc_s[...].astype(BF16)
    gd_out[...] = acc_d[...].astype(BF16)
    gr_out[...] = acc_r[...].astype(BF16)


def bucket(pack, src, dst, rel):
    width, rows = src.shape
    wide = -(-rel.shape[0] // 128) * 128
    vm = pl.BlockSpec(memory_space=pltpu.VMEM)
    return pl.pallas_call(
        bucket_kernel,
        out_shape=[
            jax.ShapeDtypeStruct((width, rows), BF16),
            jax.ShapeDtypeStruct((width, rows), BF16),
            jax.ShapeDtypeStruct((REL_ROWS, width), BF16),
        ],
        in_specs=[vm] * 4,
        out_specs=[vm] * 3,
        scratch_shapes=[
            pltpu.VMEM((width, rows), F32),
            pltpu.VMEM((width, rows), F32),
            pltpu.VMEM((REL_ROWS, width), F32),
            pltpu.VMEM((rows, TILE), BF16),
            pltpu.VMEM((wide, TILE), BF16),
            pltpu.VMEM((rows, TILE), BF16),
            pltpu.VMEM((TILES // 2, 128, rows // 128), F32),
            pltpu.VMEM((rows, width), BF16),
            pltpu.VMEM((width, wide), BF16),
        ],
        compiler_params=pltpu.CompilerParams(vmem_limit_bytes=VMEM_BYTES),
    )(pack, src, dst, rel)


class Group:
    def __init__(self, axis, size, sends, recvs):
        self.axis, self.size, self.sends, self.recvs = axis, size, sends, recvs
        self.me = lax.axis_index(axis)

    def copy(self, source, target, peer, slot):
        return pltpu.make_async_remote_copy(
            src_ref=source,
            dst_ref=target,
            send_sem=self.sends.at[peer],
            recv_sem=self.recvs.at[slot],
            device_id={self.axis: peer},
            device_id_type=MESH,
        )

    def others(self, act):
        def step(d, _):
            act(lax.rem(self.me + d, self.size))
            return 0

        lax.fori_loop(1, self.size, step, 0)

    def scatter(self, piece, slot):
        self.others(lambda p: self.copy(piece(p), slot(self.me), p, self.me).start())

    def landed(self, piece, slot):
        self.others(lambda p: self.copy(piece(p), slot(p), p, p).wait_recv())

    def sent(self, piece, slot):
        self.others(lambda p: self.copy(piece(p), slot(self.me), p, self.me).wait_send())


def meet():
    barrier = pltpu.get_barrier_semaphore()
    for axis, size in (("row", N_ROW), ("col", N_COL)):
        me = lax.axis_index(axis)

        def greet(d, _):
            peer = lax.rem(me + d, size)
            pl.semaphore_signal(barrier, inc=1, device_id={axis: peer}, device_id_type=MESH)
            return 0

        lax.fori_loop(1, size, greet, 0)
    pl.semaphore_wait(barrier, N_ROW + N_COL - 2)


def lanes(ref, width):
    return lambda i: ref.at[:, pl.ds(pl.multiple_of(i * width, width), width)]


def cuts(ref, height):
    return lambda i: ref.at[pl.ds(pl.multiple_of(i * height, height), height), :]


def own(ref):
    return lambda i: ref


def gather_kernel(src_ref, dst_ref, pack_ref, src_all, dst_all, pack_out, s1, r1, s2, r2, s3, r3):
    meet()
    cols = Group("col", N_COL, s1, r1)
    rows = Group("row", N_ROW, s2, r2)
    src_to = lanes(src_all, src_ref.shape[1])
    dst_to = lanes(dst_all, dst_ref.shape[1])
    partner = lax.rem(cols.me + HALF_COL, N_COL)
    rows.scatter(own(dst_ref), dst_to)
    cols.scatter(own(src_ref), src_to)
    swap = pltpu.make_async_remote_copy(
        src_ref=pack_ref,
        dst_ref=pack_out,
        send_sem=s3,
        recv_sem=r3,
        device_id={"col": partner},
        device_id_type=MESH,
    )
    swap.start()
    src_to(cols.me)[...] = src_ref[...]
    dst_to(rows.me)[...] = dst_ref[...]
    cols.landed(own(src_ref), src_to)
    rows.landed(own(dst_ref), dst_to)
    cols.sent(own(src_ref), src_to)
    rows.sent(own(dst_ref), dst_to)
    swap.wait()


def gather(src, dst, pack):
    vm = pl.BlockSpec(memory_space=pltpu.VMEM)
    sem = pltpu.SemaphoreType.DMA
    return pl.pallas_call(
        gather_kernel,
        out_shape=[
            jax.ShapeDtypeStruct((src.shape[0], src.shape[1] * N_COL), BF16),
            jax.ShapeDtypeStruct((dst.shape[0], dst.shape[1] * N_ROW), BF16),
            jax.ShapeDtypeStruct(pack.shape, pack.dtype),
        ],
        in_specs=[vm] * 3,
        out_specs=[vm] * 3,
        scratch_shapes=[sem((N_COL,)), sem((N_COL,)), sem((N_ROW,)), sem((N_ROW,)), sem, sem],
        compiler_params=pltpu.CompilerParams(
            collective_id=0, has_side_effects=True, vmem_limit_bytes=VMEM_BYTES
        ),
    )(src, dst, pack)


def total_of(land, size):
    total = land[0].astype(F32)
    for i in range(1, size):
        total = total + land[i].astype(F32)
    return total


def exchange_kernel(again, *refs):
    gs, gd, gr, src_ref, dst_ref = refs[:5]
    if again:
        rel_ref, his_ref, src_new, dst_new, src_all, dst_all, rel_new, his_new, g_all = refs[5:14]
        rest = refs[14:]
    else:
        src_new, dst_new, g_all = refs[5:8]
        rest = refs[8:]
    land_s, land_d, land_r, land_q = rest[:4]
    sems = rest[4:]
    meet()
    cut_s, cut_d = src_ref.shape[1], dst_ref.shape[1]
    first = Group("col", N_COL, sems[0], sems[1])
    src_sum = Group("col", N_COL, sems[2], sems[3])
    dst_sum = Group("row", N_ROW, sems[4], sems[5])
    second = Group("row", N_ROW, sems[6], sems[7])
    third = Group("col", N_COL, sems[8], sems[9])
    me_c, me_r = first.me, second.me
    slot_s, slot_d, slot_r, slot_q = land_s.at.__getitem__, land_d.at.__getitem__, land_r.at.__getitem__, land_q.at.__getitem__
    gr_cut, g_cut = cuts(gr, REL_CUT), cuts(g_all, REL_CUT)
    gs_cut, gd_cut = lanes(gs, cut_s), lanes(gd, cut_d)

    first.scatter(gr_cut, slot_r)
    dst_sum.scatter(gd_cut, slot_d)
    src_sum.scatter(gs_cut, slot_s)
    land_r[me_c] = gr_cut(me_c)[...]
    land_s[me_c] = gs_cut(me_c)[...]
    land_d[me_r] = gd_cut(me_r)[...]

    first.landed(gr_cut, slot_r)
    land_q[me_r] = total_of(land_r, N_COL).astype(BF16)
    second.scatter(lambda p: slot_q(me_r), slot_q)

    src_sum.landed(gs_cut, slot_s)
    share = src_ref[...].astype(F32) - entity_rate * total_of(land_s, N_COL)
    src_new[...] = share.astype(BF16)
    if again:
        src_to = lanes(src_all, cut_s)
        src_gather = Group("col", N_COL, sems[10], sems[11])
        src_gather.scatter(own(src_new), src_to)
        src_to(me_c)[...] = src_new[...]

    second.landed(lambda p: slot_q(me_r), slot_q)
    g_cut(me_c)[...] = total_of(land_q, N_ROW).astype(BF16)
    third.scatter(lambda p: g_cut(me_c), g_cut)

    dst_sum.landed(gd_cut, slot_d)
    share = dst_ref[...].astype(F32) - entity_rate * total_of(land_d, N_ROW)
    dst_new[...] = share.astype(BF16)
    if again:
        dst_to = lanes(dst_all, cut_d)
        dst_gather = Group("row", N_ROW, sems[12], sems[13])
        dst_gather.scatter(own(dst_new), dst_to)
        dst_to(me_r)[...] = dst_new[...]

    third.landed(lambda p: g_cut(me_c), g_cut)
    if again:
        rels = rel_ref.shape[0]
        for start in range(0, rels, CHUNK):
            at = pl.ds(start, min(CHUNK, rels - start))
            grads = g_all[at, :].astype(F32)
            history = his_ref[at, :] + grads * grads
            his_new[at, :] = history
            rel_new[at, :] = rel_ref[at, :] - relation_rate * grads / jnp.sqrt(history)
        src_gather.landed(own(src_new), src_to)
        dst_gather.landed(own(dst_new), dst_to)
        src_gather.sent(own(src_new), src_to)
        dst_gather.sent(own(dst_new), dst_to)
    first.sent(gr_cut, slot_r)
    src_sum.sent(gs_cut, slot_s)
    dst_sum.sent(gd_cut, slot_d)
    second.sent(lambda p: slot_q(me_r), slot_q)
    third.sent(lambda p: g_cut(me_c), g_cut)


def exchange(again, gs, gd, gr, src, dst, *relation):
    width = src.shape[0]
    vm = pl.BlockSpec(memory_space=pltpu.VMEM)
    sem = pltpu.SemaphoreType.DMA
    out_shape = [jax.ShapeDtypeStruct(src.shape, BF16), jax.ShapeDtypeStruct(dst.shape, BF16)]
    sizes = [N_COL, N_COL, N_COL, N_COL, N_ROW, N_ROW, N_ROW, N_ROW, N_COL, N_COL]
    if again:
        out_shape += [jax.ShapeDtypeStruct(gs.shape, BF16), jax.ShapeDtypeStruct(gd.shape, BF16)]
        out_shape += [jax.ShapeDtypeStruct(relation[0].shape, F32)] * 2
        sizes += [N_COL, N_COL, N_ROW, N_ROW]
    out_shape += [jax.ShapeDtypeStruct(gr.shape, BF16)]
    operands = (gs, gd, gr, src, dst, *relation)
    return pl.pallas_call(
        functools.partial(exchange_kernel, again),
        out_shape=out_shape,
        in_specs=[vm] * len(operands),
        out_specs=[vm] * len(out_shape),
        scratch_shapes=[
            pltpu.VMEM((N_COL, width, src.shape[1]), BF16),
            pltpu.VMEM((N_ROW, width, dst.shape[1]), BF16),
            pltpu.VMEM((N_COL, REL_CUT, width), BF16),
            pltpu.VMEM((N_ROW, REL_CUT, width), BF16),
        ]
        + [sem((n,)) for n in sizes],
        compiler_params=pltpu.CompilerParams(
            collective_id=1 if again else 2, has_side_effects=True, vmem_limit_bytes=VMEM_BYTES
        ),
    )(*operands)


def packed(src_ids, rel_ids, dst_ids, neg_ids, count):
    def rows_of(ids):
        return jnp.pad(ids.reshape(TILES, LIVE), ((0, 0), (0, TILE - LIVE)), constant_values=-1)

    live = jnp.arange(TILES * LIVE, dtype=jnp.int32) < count
    busy = jnp.broadcast_to((count + LIVE - 1) // LIVE, (TILES, TILE)).astype(jnp.int32)
    lists = [src_ids, rel_ids, jnp.where(live, dst_ids, -1), neg_ids.reshape(-1)]
    return jnp.concatenate([rows_of(ids) for ids in lists] + [busy], 0)


def on_device(
    source_table, dest_table, relations, rel_history, src_ids, rel_ids, dst_ids, neg_ids, counts
):
    src, dst = source_table[0].T, dest_table[0].T
    here, away = (
        packed(src_ids[0, 0, t], rel_ids[0, 0, t], dst_ids[0, 0, t], neg_ids[0, 0, t], counts[0, 0, t])
        for t in range(2)
    )
    src_all, dst_all, away = gather(src, dst, away)
    gs, gd, gr = bucket(here, src_all, dst_all, relations)
    src, dst, src_all, dst_all, relations, rel_history, _ = exchange(
        True, gs, gd, gr, src, dst, relations, rel_history
    )
    gs, gd, gr = bucket(away, src_all, dst_all, relations)
    src, dst, grads = exchange(False, gs, gd, gr, src, dst)
    grads = grads[: relations.shape[0]].astype(F32)
    history = rel_history + grads * grads
    relations = relations - relation_rate * grads / jnp.sqrt(history)
    return (src.T[None], dst.T[None], relations, history)


def solution(mesh):
    placed = (
        P("row", "col", None),
        P("col", "row", None),
        P(),
        P(),
        P("row", "col", None, None),
        P("row", "col", None, None),
        P("row", "col", None, None),
        P("row", "col", None, None, None),
        P("row", "col", None),
    )
    return jax.shard_map(
        on_device,
        mesh=mesh,
        in_specs=placed,
        out_specs=(P("row", "col", None), P("col", "row", None), P(), P()),
        check_vma=False,
    )
```

time: 1740 us -> 411 us (0.24)
  waiting for transfers between devices: 1060 us -> 0 us
  Pallas kernels: 0 us -> 383 us
  starting transfers between devices: 233 us -> 0 us
  other arithmetic: 189 us -> 6.79 us
  local copies, waits for them, and re-layouts: 196 us -> 17.3 us
  matrix products: 27.2 us -> 0 us
    pallas_call x0 -> x5, Pallas kernels: none -> 383 us  [the longest x2 283 us: exchange(): pl.pallas_call(functools.partial(exchange_kernel, again), out_shape=out_s...]
    psum x2 -> x0, waiting for transfers between devices: 382 us -> none  [relation_step(): total = lax.psum(grads, ('row', 'col'))]
    unnamed x12 -> x0, waiting for transfers between devices: 331 us -> none
    ppermute x2 -> x0, starting transfers between devices: 233 us -> none  [swapped(): lax.ppermute(shard, axis, [(i, i ^ 1 << bit) for i in range(lax.axis_size...]
    all_gather x4 -> x0, waiting for transfers between devices: 167 us -> none  [the longest x1 50.5 us: on_device(): partner_block = lax.all_gather(partner_share, 'row', axis=0, tiled=True)]
    reduce_scatter x2 -> x0, waiting for transfers between devices: 147 us -> none  [the longest x1 73.5 us: on_device(): lax.psum_scatter(moved.astype(jnp.float32).astype(jnp.bfloat16), 'row', s...]
    scatter-add x12 -> x0, other arithmetic: 135 us -> none  [the longest x3 34.5 us: block_terms(): grad_dst = grad_dst.at[neg_pick].add(grad_negrows)]
    gather x18 -> x0, local copies, waits for them, and re-layouts: 80.3 us -> none  [the longest x6 22.2 us: block_terms(): source = src_block[src_pick].astype(jnp.float32)]
  transfers between devices with their start and end apart: 12 -> 0, of which waited for: 12 -> 0; matrix products, arithmetic and copies ran while one was open for 3% -> 0% of each run, Pallas kernels for 0% -> 0%
where the time goes in v1:
time: 411 us; the launch traced here: 409 us
  Pallas kernels  383 us (93%)
  local copies, waits for them, and re-layouts  17.3 us (4%)
  other arithmetic  6.79 us (2%)
    pallas_call x2, Pallas kernels, exchange(): pl.pallas_call(functools.partial(exchange_kernel, again), out_shape=out_s...  283 us
    pallas_call x2, Pallas kernels, bucket(): pl.pallas_call(bucket_kernel, out_shape=[jax.ShapeDtypeStruct((width, row...  55.5 us
    pallas_call x1, Pallas kernels, gather(): pl.pallas_call(gather_kernel, out_shape=[jax.ShapeDtypeStruct((src.shape[...  44.6 us
    unnamed x28, local copies, waits for them, and re-layouts  12.7 us

profile of v1, /device:TPU:25, one launch (start us, length us, event | category | flops | bytes accessed | tf_op | source)
XLA Modules:
  0.0 408.9 jit_solution(3618613920230924509)
XLA Ops:
  0.6 1.3 fusion.9
  3.3 0.9 slice_reduce_fusion.2
  4.2 0.1 reshape_squeeze.14
  4.3 0.1 reshape_squeeze.12
  4.4 0.7 fusion.8
  5.1 0.1 reshape_reshape_squeeze.7
  5.2 0.1 reshape_reshape_squeeze.6
  5.3 1.0 slice_reduce_fusion
  6.3 0.1 squeeze.23
  6.4 0.7 fusion.6
  7.0 0.1 squeeze.21
  7.1 0.7 fusion.5
  7.8 0.1 reshape_squeeze.13
  7.9 0.0 copy-start.4
  7.9 0.1 reshape_squeeze.15
  8.1 0.0 copy-start.5
  8.1 0.0 copy-start.2
  8.1 3.5 copy.13.rel_ref.refs_5_
  11.6 0.0 copy-done.4
  11.6 0.0 copy-done.5
  11.6 0.0 copy-done.2
  11.6 2.3 copy.15.refs_6_
  13.8 44.6 %shard_map.120 = (bf16[400,2048]{1,0:T(8,128)(2,1)}, bf16[400,2048]{1,0:T(8,128)(2,1)}, s32[40,512]{1,0:T(8,128)}) custom-call(bf16[400,128]{1,0:T(8,128)(2,1)} %bitcast.16, bf16[400,256]{1,0:T(8,128)(2,1)} %bitcast.14, s32[40,512]{1,0:T(8,128)} %copy-done.4), custom_call_target="tpu_custom_call" | custom-call | tf_op jit(solution)/shard_map/pallas_call | solution.py:213
  58.5 27.7 %shard_map.121 = (bf16[400,2048]{1,0:T(8,128)(2,1)}, bf16[400,2048]{1,0:T(8,128)(2,1)}, bf16[1536,400]{1,0:T(8,128)(2,1)}) custom-call(s32[40,512]{1,0:T(8,128)} %copy-done.5, bf16[400,2048]{1,0:T(8,128)(2,1)} %get-tuple-element.23.src_ref, bf16[400,2048]{1,0:T(8,128)(2,1)} %get-tuple-element.24.dst_ref, f32[1345,400]{1,0:T(8,128)} %copy.13.rel_ref.refs_5_), custom_call_target="tpu_custom_call" | custom-call | tf_op jit(solution)/shard_map/pallas_call | solution.py:101
  86.2 159.5 %shard_map.122 = (bf16[400,128]{1,0:T(8,128)(2,1)}, bf16[400,256]{1,0:T(8,128)(2,1)}, bf16[400,2048]{1,0:T(8,128)(2,1)}, bf16[400,2048]{1,0:T(8,128)(2,1)}, f32[...) custom-call(bf16[400,2048]{1,0:T(8,128)(2,1)} %get-tuple-element.25.refs_0_, ...), custom_call_target="tpu_custom_call" | custom-call | tf_op jit(solution)/shard_map/pallas_call | solution.py:323
  245.6 27.8 %shard_map.123 = (bf16[400,2048]{1,0:T(8,128)(2,1)}, bf16[400,2048]{1,0:T(8,128)(2,1)}, bf16[1536,400]{1,0:T(8,128)(2,1)}) custom-call(s32[40,512]{1,0:T(8,128)} %get-tuple-element.22.pack_ref, bf16[400,2048]{1,0:T(8,128)(2,1)} %get-tuple-element.28.src_ref, bf16[400,2048]{1,0:T(8,128)(2,1)} %get-tuple-element.29.dst_ref, f32[1345,400]{1,0:T(8,128)} %get-tuple-element.30.rel_ref), custom_call_target="tpu_custom_call" | custom-call | tf_op jit(solution)/shard_map/pallas_call | solution.py:101
  273.4 0.0 copy-start
  273.4 123.1 %shard_map.124 = (bf16[400,128]{1,0:T(8,128)(2,1)}, bf16[400,256]{1,0:T(8,128)(2,1)}, bf16[1536,400]{1,0:T(8,128)(2,1)}) custom-call(bf16[400,2048]{1,0:T(8,128)(2,1)} %get-tuple-element.31.refs_0_, bf16[400,2048]{1,0:T(8,128)(2,1)} %get-tuple-element.32.refs_1_, bf16[1536,400]{1,0:T(8,128)(2,1)} %get-tuple-element.33.refs_2_, ...), custom_call_target="tpu_custom_call" | custom-call | tf_op jit(solution)/shard_map/pallas_call | solution.py:323
  396.5 0.0 copy-done
  396.6 5.5 %fusion.1 = (f32[1345,400]{1,0:T(8,128)}, f32[1345,400]{1,0:T(8,128)}) fusion(f32[1345,400]{1,0:T(8,128)S(1)} %copy-done, bf16[1536,400]{1,0:T(8,128)(2,1)} %get-tuple-element.38, f32[1345,400]{1,0:T(8,128)} %get-tuple-element.39), kind=kLoop, calls=%fused_computation.3 | loop fusion | flops 3228000 | bytes 9684000 | tf_op jit(solution)/shard_map/sub | solution.py:368
  402.0 0.0 copy-start.1
  402.0 3.4 copy.16
  405.4 0.0 copy-done.1
  405.4 0.0 copy-start.6
  405.4 0.0 copy-start.3
  405.4 2.1 copy.17
  407.6 0.0 copy-done.6
  407.6 0.6 copy.28
  408.2 0.0 copy-done.3
  408.2 0.7 copy.29
  (10 shorter events, 0.1 us)
Async XLA Ops:
  7.9 3.6 copy-start.4
  8.1 3.5 copy-start.5
  8.1 3.5 copy-start.2
  273.4 123.1 %copy-start = (f32[1345,400]{1,0:T(8,128)S(1)}, f32[1345,400]{1,0:T(8,128)}, u32[]{:S(2)}) copy-start(f32[1345,400]{1,0:T(8,128)} %get-tuple-element.30.rel_ref) | copy-start | bytes 6456004
  402.0 3.4 copy-start.1
  405.4 2.1 copy-start.6
  405.4 2.8 copy-start.3

commit v2 on v1

v2 whole, which is shorter than its diff:
```python
import functools
import jax
import jax.numpy as jnp
from jax import lax
from jax.experimental import pallas as pl
from jax.experimental.pallas import tpu as pltpu
from jax.sharding import PartitionSpec as P

F32, BF16 = jnp.float32, jnp.bfloat16
MESH = pl.DeviceIdType.MESH
NT = (((1,), (1,)), ((), ()))
entity_rate = 0.3
relation_rate = 0.5
N_X, N_Y = 4, 4
N_ROW, N_COL = 8, 16
HALF_COL = 8
TILE, LIVE = 512, 500
TILES = 8
CHUNK = 256
REL_HALF, REL_CUT, REL_PIECE = 208, 384, 16
REL_ROWS, REL_WIDE = 2 * REL_HALF, N_X * REL_CUT
PIECES = REL_HALF // REL_PIECE
VMEM_BYTES = 60 * 2**20


def onehot(rows, base, ids):
    at = lax.broadcasted_iota(jnp.int32, (rows, ids.shape[1]), 0) + base
    return jnp.where(at == ids, 1.0, 0.0).astype(BF16)


def bucket_kernel(
    turn, sid_ref, rid_ref, did_ref, nid_ref, count_ref, src_ref, dst_ref, rel_ref,
    gs_out, gd_out, gr_out, acc_s, acc_d, acc_r, ohs, ohr, mm, cnt, dnat, relt, lists,
):
    width, rows = src_ref.shape
    half = width // 2
    blocks = TILES // 2
    count = jnp.max(count_ref[pl.ds(turn, 1), :])
    acc_s[...] = jnp.zeros_like(acc_s)
    acc_d[...] = jnp.zeros_like(acc_d)
    acc_r[...] = jnp.zeros_like(acc_r)
    relt[...] = jnp.zeros_like(relt)
    relt[:, pl.ds(0, rel_ref.shape[1])] = rel_ref[...].astype(BF16)
    eye = onehot(CHUNK, 0, lax.broadcasted_iota(jnp.int32, (1, CHUNK), 1))
    for c in range(rows // CHUNK):
        cut = pl.ds(c * CHUNK, CHUNK)
        turned = lax.dot_general(eye, dst_ref[:, cut], NT, preferred_element_type=F32)
        dnat[cut, :] = turned.astype(BF16)
    lists[...] = jnp.full(lists.shape, -1, jnp.int32)
    lane = lax.broadcasted_iota(jnp.int32, (1, LIVE), 1)
    for t in range(TILES):
        own = pl.ds(t * LIVE, LIVE)
        lists[0, pl.ds(t, 1), pl.ds(0, LIVE)] = sid_ref[pl.ds(turn, 1), own]
        lists[1, pl.ds(t, 1), pl.ds(0, LIVE)] = rid_ref[pl.ds(turn, 1), own]
        live = lane + t * LIVE < count
        lists[2, pl.ds(t, 1), pl.ds(0, LIVE)] = jnp.where(live, did_ref[pl.ds(turn, 1), own], -1)
    for k in range(blocks):
        ids = nid_ref[pl.ds(turn * blocks + k, 1), :]
        low = onehot(128, 0, ids & 127)
        high = onehot(rows // 128, 0, ids >> 7)
        total = lax.dot_general(low, high, NT, preferred_element_type=F32)
        cnt[k] = total * (1.0 / (2 * LIVE))

    def tile(t, _):
        sid, rid, did = (lists[i, pl.ds(t, 1), :] for i in range(3))
        for c in range(rows // CHUNK):
            ohs[pl.ds(c * CHUNK, CHUNK), :] = onehot(CHUNK, c * CHUNK, sid)
        ohr[...] = onehot(REL_WIDE, 0, rid)
        alive = jnp.where(did >= 0, 0.5, 0.0)
        s = jnp.dot(src_ref[...], ohs[...], preferred_element_type=F32)
        r = jnp.dot(relt[...], ohr[...], preferred_element_type=F32)
        sre, sim, rre, rim = s[:half], s[half:], r[:half], r[half:]
        rot = jnp.concatenate([sre * rre - sim * rim, sre * rim + sim * rre], 0)
        rot = (rot * alive).astype(BF16)
        weight = cnt[t // 2]
        for c in range(rows // CHUNK):
            cut = pl.ds(c * CHUNK, CHUNK)
            lean = jnp.tanh(jnp.dot(dnat[cut, :], rot, preferred_element_type=F32))
            share = jnp.concatenate([weight[:, 2 * c : 2 * c + 1], weight[:, 2 * c + 1 : 2 * c + 2]], 0)
            hit = lax.broadcasted_iota(jnp.int32, (CHUNK, TILE), 0) + c * CHUNK == did
            slope = jnp.where(hit, share + 1, share)
            mm[cut, :] = (slope * lean + jnp.where(hit, share - 1, share)).astype(BF16)
        g = jnp.dot(dst_ref[...], mm[...], preferred_element_type=F32) * alive
        acc_d[...] += lax.dot_general(rot, mm[...], NT, preferred_element_type=F32)
        gre, gim = g[:half], g[half:]
        gs = jnp.concatenate([gre * rre + gim * rim, gim * rre - gre * rim], 0).astype(BF16)
        gr = jnp.concatenate([gre * sre + gim * sim, gim * sre - gre * sim], 0).astype(BF16)
        acc_s[...] += lax.dot_general(gs, ohs[...], NT, preferred_element_type=F32)
        acc_r[...] += lax.dot_general(gr, ohr[...], NT, preferred_element_type=F32)
        return 0

    lax.fori_loop(0, (count + LIVE - 1) // LIVE, tile, 0)
    gs_out[...] = acc_s[...].astype(BF16)
    gd_out[...] = acc_d[...].astype(BF16)
    gr_out[pl.ds(0, width), :] = acc_r[...].astype(BF16)
    gr_out[pl.ds(width, REL_ROWS - width), :] = jnp.zeros((REL_ROWS - width, REL_WIDE), BF16)


def bucket(turn, lists, src, dst, rel):
    width, rows = src.shape
    vm = pl.BlockSpec(memory_space=pltpu.VMEM)
    return pl.pallas_call(
        functools.partial(bucket_kernel, turn),
        out_shape=[
            jax.ShapeDtypeStruct((width, rows), BF16),
            jax.ShapeDtypeStruct((width, rows), BF16),
            jax.ShapeDtypeStruct((REL_ROWS, REL_WIDE), BF16),
        ],
        in_specs=[vm] * 8,
        out_specs=[vm] * 3,
        scratch_shapes=[
            pltpu.VMEM((width, rows), F32),
            pltpu.VMEM((width, rows), F32),
            pltpu.VMEM((width, REL_WIDE), F32),
            pltpu.VMEM((rows, TILE), BF16),
            pltpu.VMEM((REL_WIDE, TILE), BF16),
            pltpu.VMEM((rows, TILE), BF16),
            pltpu.VMEM((TILES // 2, 128, rows // 128), F32),
            pltpu.VMEM((rows, width), BF16),
            pltpu.VMEM((width, REL_WIDE), BF16),
            pltpu.VMEM((3, TILES, TILE), jnp.int32),
        ],
        compiler_params=pltpu.CompilerParams(vmem_limit_bytes=VMEM_BYTES),
    )(*lists, src, dst, rel)


class Place:
    def __init__(self):
        self.row, self.col = lax.axis_index("row"), lax.axis_index("col")
        self.core = lax.rem(self.col, 2)
        self.x, self.y = lax.div(self.col, 4), lax.div(self.row, 2)
        self.z_hi = lax.rem(self.row, 2)
        self.xz = lax.div(self.col, 2)
        self.yz = self.row * 2 + lax.rem(self.xz, 2)

    def sibling(self, p=None):
        return {"row": self.row, "col": self.col + 1 - 2 * self.core}

    def at_x(self, p):
        return {"row": self.row, "col": 4 * p + lax.rem(self.col, 4)}

    def at_xz(self, p):
        return {"row": self.row, "col": 2 * p + self.core}

    def at_y(self, p):
        return {"row": 2 * p + self.z_hi, "col": self.col}

    def across(self, p=None):
        return {"row": self.row + 1 - 2 * self.z_hi, "col": self.col}

    def at_yz(self, p):
        return {"row": lax.div(p, 2), "col": 4 * self.x + 2 * lax.rem(p, 2) + self.core}

    def partner(self, p=None):
        return {"row": self.row, "col": lax.rem(self.col + HALF_COL, N_COL)}


def others(me, size, act):
    def step(d, _):
        act(lax.rem(me + d, size))
        return 0

    lax.fori_loop(1, size, step, 0)


def every(size, act):
    def step(d, _):
        act(d)
        return 0

    lax.fori_loop(0, size, step, 0)


def send(source, target, sems, peer, slot, device):
    return pltpu.make_async_remote_copy(
        src_ref=source,
        dst_ref=target,
        send_sem=sems[0].at[peer],
        recv_sem=sems[1].at[slot],
        device_id=device,
        device_id_type=MESH,
    )


def meet(here, groups):
    barrier = pltpu.get_barrier_semaphore()
    for me, size, where in groups:
        others(me, size, lambda p: pl.semaphore_signal(barrier, inc=1, device_id=where(p), device_id_type=MESH))
    pl.semaphore_wait(barrier, sum(size - 1 for _, size, _ in groups))


def lanes(ref, width):
    return lambda i: ref.at[:, pl.ds(pl.multiple_of(i * width, width), width)]


class SourceGather:
    def __init__(self, here, mine, table, sems):
        self.here, self.mine, self.to = here, mine, lanes(table, mine.shape[1])
        self.far, self.near = sems[:2], sems[2:]
        self.slot = lambda p: self.to(2 * p + here.core)
        self.back = lambda p: self.to(2 * p + 1 - here.core)

    def far_copy(self, source, target, p, slot):
        return send(source, target, self.far, p, slot, self.here.at_xz(p))

    def near_copy(self, source, target, p):
        return send(source, target, self.near, p, p, self.here.sibling())

    def start(self):
        me = self.here.xz
        others(me, N_ROW, lambda p: self.far_copy(self.mine, self.slot(me), p, me).start())
        self.near_copy(self.mine, self.slot(me), me).start()
        self.slot(me)[...] = self.mine[...]

    def forward(self):
        def step(p):
            self.far_copy(self.mine, self.slot(p), p, p).wait_recv()
            self.near_copy(self.slot(p), self.slot(p), p).start()

        others(self.here.xz, N_ROW, step)

    def finish(self):
        me = self.here.xz
        every(N_ROW, lambda p: self.near_copy(self.mine, self.back(p), p).wait_recv())
        others(me, N_ROW, lambda p: self.far_copy(self.mine, self.slot(me), p, me).wait_send())
        every(N_ROW, lambda p: self.near_copy(self.mine, self.slot(p), p).wait_send())


class DestGather:
    def __init__(self, here, mine, table, sems):
        self.here, self.mine, self.to = here, mine, lanes(table, mine.shape[1])
        self.pair, self.first, self.second = sems[:2], sems[2:4], sems[4:]
        self.slot = lambda p: self.to(2 * p + here.z_hi)
        self.back = lambda p: self.to(2 * p + 1 - here.z_hi)

    def pair_copy(self, target):
        return send(self.mine, target, self.pair, 0, 0, self.here.across())

    def copy(self, sems, source, target, p, slot):
        return send(source, target, sems, p, slot, self.here.at_y(p))

    def start(self):
        me = self.here.y
        self.pair_copy(self.slot(me)).start()
        others(me, N_Y, lambda p: self.copy(self.first, self.mine, self.slot(me), p, me).start())
        self.slot(me)[...] = self.mine[...]

    def forward(self):
        me = self.here.y
        got = self.back(me)
        self.pair_copy(got).wait_recv()
        others(me, N_Y, lambda p: self.copy(self.second, got, got, p, me).start())

    def finish(self):
        me = self.here.y
        others(me, N_Y, lambda p: self.copy(self.first, self.mine, self.slot(p), p, p).wait_recv())
        others(me, N_Y, lambda p: self.copy(self.second, self.mine, self.back(p), p, p).wait_recv())
        self.pair_copy(self.slot(me)).wait_send()
        others(me, N_Y, lambda p: self.copy(self.first, self.mine, self.slot(me), p, me).wait_send())
        others(me, N_Y, lambda p: self.copy(self.second, self.mine, self.back(me), p, me).wait_send())


GATHER_SEMS = [N_ROW] * 4 + [1, 1] + [N_Y] * 4


def gather_kernel(src_ref, dst_ref, *refs):
    lists, (src_all, dst_all), swapped = refs[:5], refs[5:7], refs[7:12]
    sems = refs[12:]
    here = Place()
    meet(
        here,
        [
            (here.core, 2, here.sibling),
            (here.xz, N_ROW, here.at_xz),
            (here.y, N_Y, here.at_y),
            (here.z_hi, 2, here.across),
        ],
    )
    dst = DestGather(here, dst_ref, dst_all, sems[6:12])
    src = SourceGather(here, src_ref, src_all, sems[2:6])
    dst.start()
    src.start()
    swaps = [send(a, b, sems[:2], i, i, here.partner()) for i, (a, b) in enumerate(zip(lists, swapped))]
    for swap in swaps:
        swap.start()
    dst.forward()
    src.forward()
    dst.finish()
    src.finish()
    for swap in swaps:
        swap.wait()


def gather(src, dst, lists):
    vm = pl.BlockSpec(memory_space=pltpu.VMEM)
    sem = pltpu.SemaphoreType.DMA
    return pl.pallas_call(
        gather_kernel,
        out_shape=[
            jax.ShapeDtypeStruct((src.shape[0], src.shape[1] * N_COL), BF16),
            jax.ShapeDtypeStruct((dst.shape[0], dst.shape[1] * N_ROW), BF16),
        ]
        + [jax.ShapeDtypeStruct(a.shape, a.dtype) for a in lists],
        in_specs=[vm] * 7,
        out_specs=[vm] * 7,
        scratch_shapes=[sem((n,)) for n in [len(lists)] * 2 + GATHER_SEMS],
        compiler_params=pltpu.CompilerParams(
            collective_id=0, has_side_effects=True, vmem_limit_bytes=VMEM_BYTES
        ),
    )(src, dst, *lists)


def total_of(land, size):
    total = land[0].astype(F32)
    for i in range(1, size):
        total = total + land[i].astype(F32)
    return total


def exchange_kernel(again, *refs):
    gs, gd, gr, src_ref, dst_ref = refs[:5]
    if again:
        rel_ref, his_ref, src_new, dst_new, g_all, src_all, dst_all, rel_new, his_new = refs[5:14]
        rest = refs[14:]
    else:
        src_new, dst_new, g_all = refs[5:8]
        rest = refs[8:]
    s_near, s_part, s_far, d_across, d_own, d_part, d_last, r_near, r_part, r_far, r_chunk, r_land = rest[:12]
    sems = rest[12:]
    here = Place()
    me_x, me_y, me_u, me_q = here.x, here.y, here.xz, here.yz
    meet(
        here,
        [
            (here.core, 2, here.sibling),
            (here.xz, N_ROW, here.at_xz),
            (here.yz, N_COL, here.at_yz),
        ],
    )
    cut_s, cut_d = src_ref.shape[1], dst_ref.shape[1]
    gs_cut, gd_cut = lanes(gs, cut_s), lanes(gd, cut_d)

    def rel_cut(ref, core, x):
        down = pl.ds(pl.multiple_of(core * REL_HALF, REL_PIECE), REL_HALF)
        return ref.at[down, pl.ds(pl.multiple_of(x * REL_CUT, REL_CUT), REL_CUT)]

    def piece(ref, w, core, x):
        down = pl.ds(pl.multiple_of(core * REL_HALF + w * REL_PIECE, REL_PIECE), REL_PIECE)
        return ref.at[down, pl.ds(pl.multiple_of(x * REL_CUT, REL_CUT), REL_CUT)]

    def part(ref, w):
        return ref.at[pl.ds(pl.multiple_of(w * REL_PIECE, REL_PIECE), REL_PIECE), :]

    near_r = lambda x: send(rel_cut(gr, 1 - here.core, x), r_near.at[x], sems[0:2], x, x, here.sibling())
    far_r = lambda x, slot: send(r_part.at[x], r_far.at[slot], sems[2:4], x, slot, here.at_x(x))
    sum_r = lambda w, slot: send(part(r_chunk, w), r_land.at[slot], sems[4:6], w, slot, here.at_yz(w))
    back_r = lambda p, w: send(
        piece(g_all, w, here.core, me_x), piece(g_all, w, here.core, me_x), sems[6:8], p, w, here.at_yz(p)
    )
    wide_r = lambda p, x: send(
        rel_cut(g_all, here.core, x), rel_cut(g_all, here.core, x), sems[8:10], p, x, here.at_x(p)
    )
    last_r = lambda core, x: send(
        rel_cut(g_all, core, x), rel_cut(g_all, core, x), sems[10:12], x, x, here.sibling()
    )
    near_s = lambda u: send(gs_cut(2 * u + 1 - here.core), s_near.at[u], sems[12:14], u, u, here.sibling())
    far_s = lambda u, slot: send(s_part.at[u], s_far.at[slot], sems[14:16], u, slot, here.at_xz(u))
    far_a = lambda p, slot: send(
        gd_cut(2 * p + 1 - here.z_hi), d_across.at[slot], sems[16:18], p, slot, here.at_y(p)
    )
    far_o = lambda p, slot: send(gd_cut(2 * p + here.z_hi), d_own.at[slot], sems[18:20], p, slot, here.at_y(p))
    pair_d = send(d_part, d_last, sems[20:22], 0, 0, here.across())

    every(N_X, lambda x: near_r(x).start())
    others(me_y, N_Y, lambda p: far_a(p, me_y).start())
    others(me_y, N_Y, lambda p: far_o(p, me_y).start())
    every(N_ROW, lambda u: near_s(u).start())
    d_across[me_y] = gd_cut(2 * me_y + 1 - here.z_hi)[...]
    d_own[me_y] = gd_cut(2 * me_y + here.z_hi)[...]

    def relation_part(x):
        near_r(x).wait_recv()
        return (rel_cut(gr, here.core, x)[...].astype(F32) + r_near[x].astype(F32)).astype(BF16)

    def relation_send(x):
        r_part[x] = relation_part(x)
        far_r(x, me_x).start()

    others(me_x, N_X, relation_send)
    r_far[me_x] = relation_part(me_x)

    def source_part(u):
        near_s(u).wait_recv()
        return (gs_cut(2 * u + here.core)[...].astype(F32) + s_near[u].astype(F32)).astype(BF16)

    def source_send(u):
        s_part[u] = source_part(u)
        far_s(u, me_u).start()

    others(me_u, N_ROW, source_send)
    s_far[me_u] = source_part(me_u)

    others(me_x, N_X, lambda x: far_r(x, x).wait_recv())
    r_chunk[...] = total_of(r_far, N_X).astype(BF16)

    def piece_step(act):
        def step(w):
            @pl.when(w != me_q)
            def _():
                act(w)

        every(PIECES, step)

    piece_step(lambda w: sum_r(w, me_q).start())

    others(me_y, N_Y, lambda p: far_a(p, p).wait_recv())
    d_part[...] = total_of(d_across, N_Y).astype(BF16)
    pair_d.start()

    @pl.when(me_q < PIECES)
    def _():
        r_land[me_q] = part(r_chunk, me_q)[...]
        others(me_q, N_COL, lambda p: sum_r(me_q, p).wait_recv())
        piece(g_all, me_q, here.core, me_x)[...] = total_of(r_land, N_COL).astype(BF16)
        others(me_q, N_COL, lambda p: back_r(p, me_q).start())

    others(me_u, N_ROW, lambda u: far_s(u, u).wait_recv())
    share = src_ref[...].astype(F32) - entity_rate * total_of(s_far, N_ROW)
    src_new[...] = share.astype(BF16)
    if again:
        src_gather = SourceGather(here, src_new, src_all, sems[22:26])
        src_gather.start()

    others(me_y, N_Y, lambda p: far_o(p, p).wait_recv())
    pair_d.wait_recv()
    share = total_of(d_own, N_Y) + d_last[...].astype(F32)
    dst_new[...] = (dst_ref[...].astype(F32) - entity_rate * share).astype(BF16)
    if again:
        dst_gather = DestGather(here, dst_new, dst_all, sems[26:32])
        dst_gather.start()

    piece_step(lambda w: back_r(w, w).wait_recv())
    others(me_x, N_X, lambda p: wide_r(p, me_x).start())
    last_r(here.core, me_x).start()
    if again:
        dst_gather.forward()

    def relation_forward(x):
        wide_r(x, x).wait_recv()
        last_r(here.core, x).start()

    others(me_x, N_X, relation_forward)
    if again:
        src_gather.forward()
    every(N_X, lambda x: last_r(1 - here.core, x).wait_recv())
    if again:
        width, rels = rel_ref.shape
        for start in range(0, rels, CHUNK):
            at = pl.ds(start, min(CHUNK, rels - start))
            grads = g_all[pl.ds(0, width), at].astype(F32)
            history = his_ref[:, at] + grads * grads
            his_new[:, at] = history
            rel_new[:, at] = rel_ref[:, at] - relation_rate * grads / jnp.sqrt(history)
        src_gather.finish()
        dst_gather.finish()

    every(N_X, lambda x: near_r(x).wait_send())
    others(me_x, N_X, lambda x: far_r(x, me_x).wait_send())
    piece_step(lambda w: sum_r(w, me_q).wait_send())

    @pl.when(me_q < PIECES)
    def _():
        others(me_q, N_COL, lambda p: back_r(p, me_q).wait_send())

    others(me_x, N_X, lambda p: wide_r(p, me_x).wait_send())
    every(N_X, lambda x: last_r(here.core, x).wait_send())
    every(N_ROW, lambda u: near_s(u).wait_send())
    others(me_u, N_ROW, lambda u: far_s(u, me_u).wait_send())
    others(me_y, N_Y, lambda p: far_a(p, me_y).wait_send())
    others(me_y, N_Y, lambda p: far_o(p, me_y).wait_send())
    pair_d.wait_send()


def exchange(again, gs, gd, gr, src, dst, *relation):
    width, cut_s, cut_d = src.shape[0], src.shape[1], dst.shape[1]
    vm = pl.BlockSpec(memory_space=pltpu.VMEM)
    sem = pltpu.SemaphoreType.DMA
    out_shape = [jax.ShapeDtypeStruct(a.shape, BF16) for a in (src, dst, gr)]
    sizes = [N_X] * 4 + [N_COL] * 4 + [N_X] * 4 + [N_ROW] * 4 + [N_Y] * 4 + [1, 1]
    if again:
        out_shape += [jax.ShapeDtypeStruct(a.shape, a.dtype) for a in (gs, gd, *relation)]
        sizes += GATHER_SEMS
    operands = (gs, gd, gr, src, dst, *relation)
    return pl.pallas_call(
        functools.partial(exchange_kernel, again),
        out_shape=out_shape,
        in_specs=[vm] * len(operands),
        out_specs=[vm] * len(out_shape),
        scratch_shapes=[
            pltpu.VMEM((N_ROW, width, cut_s), BF16),
            pltpu.VMEM((N_ROW, width, cut_s), BF16),
            pltpu.VMEM((N_ROW, width, cut_s), BF16),
            pltpu.VMEM((N_Y, width, cut_d), BF16),
            pltpu.VMEM((N_Y, width, cut_d), BF16),
            pltpu.VMEM((width, cut_d), BF16),
            pltpu.VMEM((width, cut_d), BF16),
            pltpu.VMEM((N_X, REL_HALF, REL_CUT), BF16),
            pltpu.VMEM((N_X, REL_HALF, REL_CUT), BF16),
            pltpu.VMEM((N_X, REL_HALF, REL_CUT), BF16),
            pltpu.VMEM((REL_HALF, REL_CUT), BF16),
            pltpu.VMEM((N_COL, REL_PIECE, REL_CUT), BF16),
        ]
        + [sem((n,)) for n in sizes],
        compiler_params=pltpu.CompilerParams(
            collective_id=1 if again else 2, has_side_effects=True, vmem_limit_bytes=VMEM_BYTES
        ),
    )(*operands)


def on_device(
    source_table, dest_table, relations, rel_history, src_ids, rel_ids, dst_ids, neg_ids, counts
):
    src, dst = source_table[0].T, dest_table[0].T
    rel, history = relations.T, rel_history.T
    blocks, negs = neg_ids.shape[3:]
    count = jnp.broadcast_to(counts[0, 0][:, None], (2, 128))
    here = [src_ids[0, 0], rel_ids[0, 0], dst_ids[0, 0], neg_ids[0, 0].reshape(2 * blocks, negs), count]
    src_all, dst_all, *away = gather(src, dst, here)
    gs, gd, gr = bucket(0, here, src_all, dst_all, rel)
    src, dst, _, src_all, dst_all, rel, history = exchange(True, gs, gd, gr, src, dst, rel, history)
    gs, gd, gr = bucket(1, away, src_all, dst_all, rel)
    src, dst, grads = exchange(False, gs, gd, gr, src, dst)
    grads = grads[: rel.shape[0], : rel.shape[1]].astype(F32)
    history = history + grads * grads
    rel = rel - relation_rate * grads / jnp.sqrt(history)
    return (src.T[None], dst.T[None], rel.T, history.T)


def solution(mesh):
    placed = (
        P("row", "col", None),
        P("col", "row", None),
        P(),
        P(),
        P("row", "col", None, None),
        P("row", "col", None, None),
        P("row", "col", None, None),
        P("row", "col", None, None, None),
        P("row", "col", None),
    )
    return jax.shard_map(
        on_device,
        mesh=mesh,
        in_specs=placed,
        out_specs=(P("row", "col", None), P("col", "row", None), P(), P()),
        check_vma=False,
    )
```

time: 411 us -> 256 us (0.62)
  Pallas kernels: 383 us -> 246 us
  local copies, waits for them, and re-layouts: 17.3 us -> 4 us
    pallas_call x2, Pallas kernels: 283 us -> 166 us  [exchange(): pl.pallas_call(functools.partial(exchange_kernel, again), out_shape=out_s...]
    pallas_call x1, Pallas kernels: 44.6 us -> 26.2 us  [gather(): pl.pallas_call(gather_kernel, out_shape=[jax.ShapeDtypeStruct((src.shape[...]
    unnamed x28 -> x8, local copies, waits for them, and re-layouts: 12.7 us -> 1.33 us
    sub x1 -> x0, other arithmetic: 5.48 us -> none  [on_device(): relations = relations - relation_rate * grads / jnp.sqrt(history)]
    transpose x0 -> x1, other arithmetic: none -> 4.59 us  [on_device(): return (src.T[None], dst.T[None], rel.T, history.T)]
where the time goes in v2:
time: 256 us
  Pallas kernels  246 us (96%)
  other arithmetic  4.59 us (2%)
  local copies, waits for them, and re-layouts  4 us (2%)
    pallas_call x2, Pallas kernels, exchange(): pl.pallas_call(functools.partial(exchange_kernel, again), out_shape=out_s...  166 us
    pallas_call x2, Pallas kernels, bucket(): pl.pallas_call(functools.partial(bucket_kernel, turn), out_shape=[jax.Sha...  53.8 us
    pallas_call x1, Pallas kernels, gather(): pl.pallas_call(gather_kernel, out_shape=[jax.ShapeDtypeStruct((src.shape[...  26.2 us

profile of v2, /device:TPU:25, one launch (start us, length us, event | category | flops | bytes accessed | tf_op | source)
XLA Modules:
  0.0 255.7 jit_solution(14631343467375498600)
XLA Ops:
  0.6 1.3 broadcast_in_dim.14.refs_4_.count_ref
  1.9 1.4 reshape_squeeze.3.refs_3_.nid_ref
  3.3 26.2 %shard_map.120 = (bf16[400,2048]{1,0:T(8,128)(2,1)}, bf16[400,2048]{1,0:T(8,128)(2,1)}, s32[2,4000]{1,0:T(2,128)}, s32[2,4000]{1,0:T(2,128)}, s32[2,4000]{1,0:T(...) custom-call(bf16[400,128]{1,0:T(8,128)(2,1)} %bitcast.27, bf16[400,256]{1,0:T(8,128)(2,1)} %bitcast.25, s32[2,4000]{1,0:T(2,128)} %bitcast.30, ...), custom_call_target="tpu_custom_call" | custom-call | tf_op jit(solution)/shard_map/pallas_call | solution.py:297
  29.5 20.2 %shard_map.121 = (bf16[400,2048]{1,0:T(8,128)(2,1)}, bf16[400,2048]{1,0:T(8,128)(2,1)}, bf16[416,1536]{1,0:T(8,128)(2,1)}) custom-call(s32[2,4000]{1,0:T(2,128)} %bitcast.31, s32[2,4000]{1,0:T(2,128)} %bitcast.33, s32[2,4000]{1,0:T(2,128)} %bitcast.35, s32[8,1000]{1,0:T(8,128)} %reshape_squeeze.3.refs_3_.nid_ref, ...), custom_call_target="tpu_custom_call" | custom-call | tf_op jit(solution)/shard_map/pallas_call | solution.py:102
  49.7 102.1 %shard_map.122 = (bf16[400,128]{1,0:T(8,128)(2,1)}, bf16[400,256]{1,0:T(8,128)(2,1)}, bf16[416,1536]{1,0:T(8,128)(2,1)}, bf16[400,2048]{1,0:T(8,128)(2,1)}, bf16...) custom-call(bf16[400,2048]{1,0:T(8,128)(2,1)} %get-tuple-element.33.refs_0_, ...), custom_call_target="tpu_custom_call" | custom-call | tf_op jit(solution)/shard_map/pallas_call | solution.py:494
  151.8 33.6 %shard_map.123 = (bf16[400,2048]{1,0:T(8,128)(2,1)}, bf16[400,2048]{1,0:T(8,128)(2,1)}, bf16[416,1536]{1,0:T(8,128)(2,1)}) custom-call(s32[2,4000]{1,0:T(2,128)} %get-tuple-element.26.sid_ref, s32[2,4000]{1,0:T(2,128)} %get-tuple-element.27.rid_ref, s32[2,4000]{1,0:T(2,128)} %get-tuple-element.28.did_ref, s32[8,1000]{1,0:T(8,128)} %get-tuple-element.29.nid_ref, ...), custom_call_target="tpu_custom_call" | custom-call | tf_op jit(solution)/shard_map/pallas_call | solution.py:102
  185.4 0.0 copy-start
  185.4 64.3 %shard_map.124 = (bf16[400,128]{1,0:T(8,128)(2,1)}, bf16[400,256]{1,0:T(8,128)(2,1)}, bf16[416,1536]{1,0:T(8,128)(2,1)}) custom-call(bf16[400,2048]{1,0:T(8,128)(2,1)} %get-tuple-element.39.refs_0_, bf16[400,2048]{1,0:T(8,128)(2,1)} %get-tuple-element.40.refs_1_, bf16[416,1536]{1,0:T(8,128)(2,1)} %get-tuple-element.41.refs_2_, ...), custom_call_target="tpu_custom_call" | custom-call | tf_op jit(solution)/shard_map/pallas_call | solution.py:494
  249.7 0.0 copy-done
  249.7 0.0 copy-start.2
  249.8 0.0 copy-start.1
  249.8 4.6 %fusion.4 = (f32[1345,400]{0,1:T(8,128)}, f32[1345,400]{0,1:T(8,128)}) fusion(f32[400,1345]{1,0:T(8,128)} %get-tuple-element.47, bf16[416,1536]{1,0:T(8,128)(2,1)} %get-tuple-element.46, f32[400,1345]{1,0:T(8,128)S(1)} %copy-done), kind=kLoop, calls=%fused_computation.6 | loop fusion | flops 3228000 | bytes 9684000 | tf_op jit(solution)/shard_map/transpose | solution.py:536
  254.4 0.0 copy-done.2
  254.4 0.6 copy.15
  255.0 0.0 copy-done.1
  255.0 0.7 copy.16
Async XLA Ops:
  185.4 64.4 %copy-start = (f32[400,1345]{1,0:T(8,128)S(1)}, f32[400,1345]{1,0:T(8,128)}, u32[]{:S(2)}) copy-start(f32[400,1345]{1,0:T(8,128)} %get-tuple-element.38.rel_ref) | copy-start | bytes 6456004
  249.7 4.6 %copy-start.2 = (bf16[400,128]{1,0:T(8,128)(2,1)S(1)}, bf16[400,128]{1,0:T(8,128)(2,1)}, u32[]{:S(2)}) copy-start(bf16[400,128]{1,0:T(8,128)(2,1)} %get-tuple-element.44) | copy-start | bytes 307204
  249.8 5.3 %copy-start.1 = (bf16[400,256]{1,0:T(8,128)(2,1)S(1)}, bf16[400,256]{1,0:T(8,128)(2,1)}, u32[]{:S(2)}) copy-start(bf16[400,256]{1,0:T(8,128)(2,1)} %get-tuple-element.45) | copy-start | bytes 614404

commit v3 on v0

v3 whole, which is shorter than its diff:
```python
import functools
import jax
import jax.numpy as jnp
from jax import lax
from jax.experimental import pallas as pl
from jax.experimental.pallas import tpu as pltpu
from jax.sharding import PartitionSpec as P

F32, BF16 = jnp.float32, jnp.bfloat16
MESH = pl.DeviceIdType.MESH
NT = (((1,), (1,)), ((), ()))
entity_rate = 0.3
relation_rate = 0.5
N_X, N_Y = 4, 4
N_ROW, N_COL = 8, 16
HALF_COL = 8
TILE, LIVE = 512, 500
TILES = 8
CHUNK, PAIR = 256, 512
SLOTS = TILES * TILE
REL_HALF, REL_CUT, REL_PIECE = 208, 384, 16
REL_ROWS, REL_WIDE = 2 * REL_HALF, N_X * REL_CUT
PIECES = REL_HALF // REL_PIECE
VMEM_BYTES = 60 * 2**20


class Place:
    def __init__(self):
        self.row, self.col = lax.axis_index("row"), lax.axis_index("col")
        self.core = lax.rem(self.col, 2)
        self.x, self.y = lax.div(self.col, 4), lax.div(self.row, 2)
        self.z_hi = lax.rem(self.row, 2)
        self.xz = lax.div(self.col, 2)
        self.yz = self.row * 2 + lax.rem(self.xz, 2)

    def sibling(self, p=None):
        return {"row": self.row, "col": self.col + 1 - 2 * self.core}

    def at_x(self, p):
        return {"row": self.row, "col": 4 * p + lax.rem(self.col, 4)}

    def at_xz(self, p):
        return {"row": self.row, "col": 2 * p + self.core}

    def at_y(self, p):
        return {"row": 2 * p + self.z_hi, "col": self.col}

    def across(self, p=None):
        return {"row": self.row + 1 - 2 * self.z_hi, "col": self.col}

    def at_yz(self, p):
        return {"row": lax.div(p, 2), "col": 4 * self.x + 2 * lax.rem(p, 2) + self.core}

    def partner(self, p=None):
        return {"row": self.row, "col": lax.rem(self.col + HALF_COL, N_COL)}


def others(me, size, act):
    def step(d, _):
        act(lax.rem(me + d, size))
        return 0

    lax.fori_loop(1, size, step, 0)


def every(size, act):
    def step(d, _):
        act(d)
        return 0

    lax.fori_loop(0, size, step, 0)


def send(source, target, sems, peer, slot, device):
    return pltpu.make_async_remote_copy(
        src_ref=source,
        dst_ref=target,
        send_sem=sems[0].at[peer],
        recv_sem=sems[1].at[slot],
        device_id=device,
        device_id_type=MESH,
    )


def meet(here, groups):
    barrier = pltpu.get_barrier_semaphore()
    for me, size, where in groups:
        others(me, size, lambda p: pl.semaphore_signal(barrier, inc=1, device_id=where(p), device_id_type=MESH))
    pl.semaphore_wait(barrier, sum(size - 1 for _, size, _ in groups))


def lanes(ref, width):
    return lambda i: ref.at[:, pl.ds(pl.multiple_of(i * width, width), width)]


class SourceGather:
    def __init__(self, here, mine, table, sems):
        self.here, self.mine, self.to = here, mine, lanes(table, mine.shape[1])
        self.far, self.near = sems[:2], sems[2:]
        self.slot = lambda p: self.to(2 * p + here.core)
        self.back = lambda p: self.to(2 * p + 1 - here.core)

    def far_copy(self, source, target, p, slot):
        return send(source, target, self.far, p, slot, self.here.at_xz(p))

    def near_copy(self, source, target, p):
        return send(source, target, self.near, p, p, self.here.sibling())

    def start(self):
        me = self.here.xz
        others(me, N_ROW, lambda p: self.far_copy(self.mine, self.slot(me), p, me).start())
        self.near_copy(self.mine, self.slot(me), me).start()
        self.slot(me)[...] = self.mine[...]

    def forward(self):
        def step(p):
            self.far_copy(self.mine, self.slot(p), p, p).wait_recv()
            self.near_copy(self.slot(p), self.slot(p), p).start()

        others(self.here.xz, N_ROW, step)

    def arrive(self):
        every(N_ROW, lambda p: self.near_copy(self.mine, self.back(p), p).wait_recv())

    def drain(self):
        me = self.here.xz
        others(me, N_ROW, lambda p: self.far_copy(self.mine, self.slot(me), p, me).wait_send())
        every(N_ROW, lambda p: self.near_copy(self.mine, self.slot(p), p).wait_send())


class DestGather:
    def __init__(self, here, mine, table, sems):
        self.here, self.mine, self.to = here, mine, lanes(table, mine.shape[1])
        self.pair, self.first, self.second = sems[:2], sems[2:4], sems[4:]
        self.slot = lambda p: self.to(2 * p + here.z_hi)
        self.back = lambda p: self.to(2 * p + 1 - here.z_hi)

    def pair_copy(self, target):
        return send(self.mine, target, self.pair, 0, 0, self.here.across())

    def copy(self, sems, source, target, p, slot):
        return send(source, target, sems, p, slot, self.here.at_y(p))

    def start(self):
        me = self.here.y
        self.pair_copy(self.slot(me)).start()
        others(me, N_Y, lambda p: self.copy(self.first, self.mine, self.slot(me), p, me).start())
        self.slot(me)[...] = self.mine[...]

    def forward(self):
        me = self.here.y
        got = self.back(me)
        self.pair_copy(got).wait_recv()
        others(me, N_Y, lambda p: self.copy(self.second, got, got, p, me).start())

    def arrive(self, p):
        self.copy(self.first, self.mine, self.slot(p), p, p).wait_recv()
        self.copy(self.second, self.mine, self.back(p), p, p).wait_recv()

    def drain(self):
        me = self.here.y
        self.pair_copy(self.slot(me)).wait_send()
        others(me, N_Y, lambda p: self.copy(self.first, self.mine, self.slot(me), p, me).wait_send())
        others(me, N_Y, lambda p: self.copy(self.second, self.mine, self.back(me), p, me).wait_send())


def onehot(rows, base, ids):
    at = lax.broadcasted_iota(jnp.int32, (rows, ids.shape[1]), 0) + base
    return jnp.where(at == ids, 1.0, 0.0).astype(BF16)


def total_of(land, size):
    total = land[0].astype(F32)
    for i in range(1, size):
        total = total + land[i].astype(F32)
    return total


def tile_at(t, size=TILE):
    return pl.ds(pl.multiple_of(t * size, size), size)


SCRATCH = dict(
    src_all=lambda w: pltpu.VMEM((w, 2048), BF16),
    dst_all=lambda w: pltpu.VMEM((w, 2048), BF16),
    dnat=lambda w: pltpu.VMEM((PAIR, w), BF16),
    relt=lambda w: pltpu.VMEM((w, REL_WIDE), BF16),
    s_all=lambda w: pltpu.VMEM((TILES, 2, w // 2, TILE), BF16),
    r_all=lambda w: pltpu.VMEM((TILES, 2, w // 2, TILE), BF16),
    rot=lambda w: pltpu.VMEM((w, SLOTS), BF16),
    gr_all=lambda w: pltpu.VMEM((w, SLOTS), BF16),
    g=lambda w: pltpu.VMEM((w, SLOTS), F32),
    mm=lambda w: pltpu.VMEM((PAIR, SLOTS), BF16),
    cnt=lambda w: pltpu.VMEM((TILES // 2, 2048, 128), F32),
    ohs=lambda w: pltpu.VMEM((2048, TILE), BF16),
    ohr=lambda w: pltpu.VMEM((REL_WIDE, TILE), BF16),
    lists=lambda w: pltpu.VMEM((8, SLOTS), jnp.int32),
    gd=lambda w: pltpu.VMEM((w, 2048), BF16),
    gs=lambda w: pltpu.VMEM((w, 2048), BF16),
    gr=lambda w: pltpu.VMEM((REL_ROWS, REL_WIDE), BF16),
    g_all=lambda w: pltpu.VMEM((REL_ROWS, REL_WIDE), BF16),
    s_near=lambda w: pltpu.VMEM((N_ROW, w, 128), BF16),
    s_part=lambda w: pltpu.VMEM((N_ROW, w, 128), BF16),
    s_far=lambda w: pltpu.VMEM((N_ROW, w, 128), BF16),
    d_across=lambda w: pltpu.VMEM((N_Y, w, 256), BF16),
    d_own=lambda w: pltpu.VMEM((N_Y, w, 256), BF16),
    d_part=lambda w: pltpu.VMEM((w, 256), BF16),
    d_last=lambda w: pltpu.VMEM((w, 256), BF16),
    r_near=lambda w: pltpu.VMEM((N_X, REL_HALF, REL_CUT), BF16),
    r_part=lambda w: pltpu.VMEM((N_X, REL_HALF, REL_CUT), BF16),
    r_far=lambda w: pltpu.VMEM((N_X, REL_HALF, REL_CUT), BF16),
    r_chunk=lambda w: pltpu.VMEM((REL_HALF, REL_CUT), BF16),
    r_land=lambda w: pltpu.VMEM((N_COL, REL_PIECE, REL_CUT), BF16),
)
SEMS = dict(
    swap=5, near_r=N_X, far_r=N_X, sum_r=N_COL, back_r=N_COL, wide_r=N_X, last_r=N_X, near_s=N_ROW, far_s=N_ROW,
    far_a=N_Y, far_o=N_Y, pair_d=1, src_far=N_ROW, src_near=N_ROW, dst_pair=1, dst_first=N_Y, dst_second=N_Y,
)


class Refs:
    pass


def kernel(*refs):
    refs = list(refs)
    k = Refs()
    for name in ("src", "dst"):
        setattr(k, name, refs.pop(0))
    lists_here = [refs.pop(0) for _ in range(5)]
    rel_in, his_in = refs.pop(0), refs.pop(0)
    for name in ("src_new", "dst_new", "rel", "his"):
        setattr(k, name, refs.pop(0))
    lists_away = [refs.pop(0) for _ in range(5)]
    for name in SCRATCH:
        setattr(k, name, refs.pop(0))
    sems = {name: (refs.pop(0), refs.pop(0)) for name in SEMS}
    load_sems = refs.pop(0)
    width = k.src.shape[0]
    half = width // 2
    rels = rel_in.shape[1]
    here = Place()
    me_x, me_y, me_u, me_q = here.x, here.y, here.xz, here.yz

    loads = [pltpu.make_async_copy(a, b, load_sems.at[i]) for i, (a, b) in enumerate([(rel_in, k.rel), (his_in, k.his)])]
    for load in loads:
        load.start()
    meet(here, [(here.core, 2, here.sibling), (me_u, N_ROW, here.at_xz), (me_q, N_COL, here.at_yz)])
    gathers = []
    for src, dst in ((k.src, k.dst), (k.src_new, k.dst_new)):
        gathers.append((
            SourceGather(here, src, k.src_all, sems["src_far"] + sems["src_near"]),
            DestGather(here, dst, k.dst_all, sems["dst_pair"] + sems["dst_first"] + sems["dst_second"]),
        ))
    src_gather, dst_gather = gathers[0]
    dst_gather.start()
    src_gather.start()
    swaps = [send(a, b, sems["swap"], i, i, here.partner()) for i, (a, b) in enumerate(zip(lists_here, lists_away))]
    for swap in swaps:
        swap.start()


    gs_cut, gd_cut = lanes(k.gs, 128), lanes(k.gd, 256)

    def rel_cut(ref, core, x):
        down = pl.ds(pl.multiple_of(core * REL_HALF, REL_PIECE), REL_HALF)
        return ref.at[down, pl.ds(pl.multiple_of(x * REL_CUT, REL_CUT), REL_CUT)]

    def piece(ref, w, core, x):
        down = pl.ds(pl.multiple_of(core * REL_HALF + w * REL_PIECE, REL_PIECE), REL_PIECE)
        return ref.at[down, pl.ds(pl.multiple_of(x * REL_CUT, REL_CUT), REL_CUT)]

    def part(ref, w):
        return ref.at[pl.ds(pl.multiple_of(w * REL_PIECE, REL_PIECE), REL_PIECE), :]

    def same(ref, name, peer, slot, device):
        return send(ref, ref, sems[name], peer, slot, device)

    near_r = lambda x: send(rel_cut(k.gr, 1 - here.core, x), k.r_near.at[x], sems["near_r"], x, x, here.sibling())
    far_r = lambda x, slot: send(k.r_part.at[x], k.r_far.at[slot], sems["far_r"], x, slot, here.at_x(x))
    sum_r = lambda w, slot: send(part(k.r_chunk, w), k.r_land.at[slot], sems["sum_r"], w, slot, here.at_yz(w))
    back_r = lambda p, w: same(piece(k.g_all, w, here.core, me_x), "back_r", p, w, here.at_yz(p))
    wide_r = lambda p, x: same(rel_cut(k.g_all, here.core, x), "wide_r", p, x, here.at_x(p))
    last_r = lambda core, x: same(rel_cut(k.g_all, core, x), "last_r", x, x, here.sibling())
    near_s = lambda u: send(gs_cut(2 * u + 1 - here.core), k.s_near.at[u], sems["near_s"], u, u, here.sibling())
    far_s = lambda u, slot: send(k.s_part.at[u], k.s_far.at[slot], sems["far_s"], u, slot, here.at_xz(u))
    far_a = lambda p, slot: send(
        gd_cut(2 * p + 1 - here.z_hi), k.d_across.at[slot], sems["far_a"], p, slot, here.at_y(p)
    )
    far_o = lambda p, slot: send(gd_cut(2 * p + here.z_hi), k.d_own.at[slot], sems["far_o"], p, slot, here.at_y(p))
    pair_d = send(k.d_part, k.d_last, sems["pair_d"], 0, 0, here.across())

    def piece_step(act):
        def step(w):
            @pl.when(w != me_q)
            def _():
                act(w)

        every(PIECES, step)


    def read_lists(turn, sid, rid, did, nid, count):
        k.lists[...] = jnp.full(k.lists.shape, -1, jnp.int32)
        limit = count[pl.ds(turn, 1), pl.ds(0, LIVE)]
        lane = lax.broadcasted_iota(jnp.int32, (1, LIVE), 1)
        for t in range(TILES):
            own, to = pl.ds(t * LIVE, LIVE), pl.ds(t * TILE, LIVE)
            k.lists[pl.ds(0, 1), to] = sid[pl.ds(turn, 1), own]
            k.lists[pl.ds(1, 1), to] = rid[pl.ds(turn, 1), own]
            k.lists[pl.ds(2, 1), to] = jnp.where(lane + t * LIVE < limit, did[pl.ds(turn, 1), own], -1)
        blocks = TILES // 2
        for b in range(blocks):
            ids = nid[pl.ds(turn * blocks + b, 1), :]
            low = onehot(128, 0, ids & 127)
            high = onehot(16, 0, ids >> 7)
            total = lax.dot_general(low, high, NT, preferred_element_type=F32) * (1.0 / (2 * LIVE))
            for h in range(16):
                k.cnt[b, pl.ds(h * 128, 128), :] = jnp.broadcast_to(total[:, h : h + 1], (128, 128))

    def cast_relations():
        k.relt[...] = jnp.zeros_like(k.relt)
        k.relt[:, pl.ds(0, rels)] = k.rel[...].astype(BF16)

    def pick_relations():
        def step(t):
            k.ohr[...] = onehot(REL_WIDE, 0, k.lists[pl.ds(1, 1), tile_at(t)])
            r = jnp.dot(k.relt[...], k.ohr[...], preferred_element_type=F32).astype(BF16)
            k.r_all[t, 0] = r[:half]
            k.r_all[t, 1] = r[half:]

        every(TILES, step)

    def pick_sources():
        def step(t):
            sid = k.lists[pl.ds(0, 1), tile_at(t)]
            alive = jnp.where(k.lists[pl.ds(2, 1), tile_at(t)] >= 0, 0.5, 0.0)
            for c in range(2048 // CHUNK):
                k.ohs[pl.ds(c * CHUNK, CHUNK), :] = onehot(CHUNK, c * CHUNK, sid)
            s = jnp.dot(k.src_all[...], k.ohs[...], preferred_element_type=F32)
            sre, sim = s[:half], s[half:]
            rre, rim = k.r_all[t, 0].astype(F32), k.r_all[t, 1].astype(F32)
            k.s_all[t, 0] = sre.astype(BF16)
            k.s_all[t, 1] = sim.astype(BF16)
            rot = jnp.concatenate([sre * rre - sim * rim, sre * rim + sim * rre], 0)
            k.rot[:, tile_at(t)] = (rot * alive).astype(BF16)
            k.g[:, tile_at(t)] = jnp.zeros((width, TILE), F32)

        every(TILES, step)

    def score(dst_gather):
        eye = onehot(CHUNK, 0, lax.broadcasted_iota(jnp.int32, (1, CHUNK), 1))

        def pair_step(d):
            y = lax.rem(me_y + d, N_Y)

            @pl.when(d > 0)
            def _():
                dst_gather.arrive(y)

            for h in range(2):
                some = k.dst_all[:, pl.ds(pl.multiple_of(y * PAIR + h * CHUNK, CHUNK), CHUNK)]
                turned = lax.dot_general(eye, some, NT, preferred_element_type=F32)
                k.dnat[pl.ds(h * CHUNK, CHUNK), :] = turned.astype(BF16)

            def step(t):
                did = k.lists[pl.ds(2, 1), tile_at(t)]
                rot = k.rot[:, tile_at(t)]
                for h in range(2):
                    down = pl.ds(h * CHUNK, CHUNK)
                    base = y * PAIR + h * CHUNK
                    lean = jnp.tanh(jnp.dot(k.dnat[down, :], rot, preferred_element_type=F32))
                    share = k.cnt[lax.div(t, 2), pl.ds(pl.multiple_of(base, CHUNK), CHUNK), :]
                    share = jnp.concatenate([share] * (TILE // 128), 1)
                    hit = lax.broadcasted_iota(jnp.int32, (CHUNK, TILE), 0) + base == did
                    slope = jnp.where(hit, share + 1, share)
                    k.mm[down, tile_at(t)] = (slope * lean + jnp.where(hit, share - 1, share)).astype(BF16)
                k.g[:, tile_at(t)] += jnp.dot(
                    k.dst_all[:, tile_at(y, PAIR)], k.mm[:, tile_at(t)], preferred_element_type=F32
                )

            every(TILES, step)
            total = lax.dot_general(k.rot[...], k.mm[...], NT, preferred_element_type=F32)
            k.gd[:, tile_at(y, PAIR)] = total.astype(BF16)

            @pl.when(d > 0)
            def _():
                far_a(y, me_y).start()
                far_o(y, me_y).start()

        every(N_Y, pair_step)
        k.d_across[me_y] = gd_cut(2 * me_y + 1 - here.z_hi)[...]
        k.d_own[me_y] = gd_cut(2 * me_y + here.z_hi)[...]

    def edge_grads():
        def step(t):
            alive = jnp.where(k.lists[pl.ds(2, 1), tile_at(t)] >= 0, 0.5, 0.0)
            g = k.g[:, tile_at(t)] * alive
            gre, gim = g[:half], g[half:]
            sre, sim = k.s_all[t, 0].astype(F32), k.s_all[t, 1].astype(F32)
            rre, rim = k.r_all[t, 0].astype(F32), k.r_all[t, 1].astype(F32)
            k.rot[:, tile_at(t)] = jnp.concatenate([gre * rre + gim * rim, gim * rre - gre * rim], 0).astype(BF16)
            k.gr_all[:, tile_at(t)] = jnp.concatenate([gre * sre + gim * sim, gim * sre - gre * sim], 0).astype(BF16)

        every(TILES, step)

    def spread(grads, row, base):
        for t in range(TILES):
            k.mm[:, pl.ds(t * TILE, TILE)] = onehot(PAIR, base, k.lists[pl.ds(row, 1), pl.ds(t * TILE, TILE)])
        return lax.dot_general(grads[...], k.mm[...], NT, preferred_element_type=F32).astype(BF16)

    def spread_relations():
        k.gr[pl.ds(width, REL_ROWS - width), :] = jnp.zeros((REL_ROWS - width, REL_WIDE), BF16)

        def step(c):
            k.gr[pl.ds(0, width), tile_at(c, PAIR)] = spread(k.gr_all, 1, c * PAIR)

            @pl.when(c < 2)
            def _():
                near_r(c).start()

            @pl.when(c == 2)
            def _():
                near_r(2).start()
                near_r(3).start()

        every(REL_WIDE // PAIR, step)

    def spread_sources(first, last):
        def step(c):
            k.gs[:, tile_at(c, PAIR)] = spread(k.rot, 0, c * PAIR)
            near_s(2 * c).start()
            near_s(2 * c + 1).start()
            return 0

        lax.fori_loop(first, last, lambda c, _: step(c), 0)

    def relation_part(x):
        near_r(x).wait_recv()
        return (rel_cut(k.gr, here.core, x)[...].astype(F32) + k.r_near[x].astype(F32)).astype(BF16)

    def relation_send(x):
        k.r_part[x] = relation_part(x)
        far_r(x, me_x).start()

    def source_part(u):
        near_s(u).wait_recv()
        return (gs_cut(2 * u + here.core)[...].astype(F32) + k.s_near[u].astype(F32)).astype(BF16)

    def source_send(u):
        k.s_part[u] = source_part(u)
        far_s(u, me_u).start()

    def relation_forward(x):
        wide_r(x, x).wait_recv()
        last_r(here.core, x).start()

    def reduce(src, dst, again):
        edge_grads()
        spread_relations()
        spread_sources(0, 1)
        others(me_x, N_X, relation_send)
        k.r_far[me_x] = relation_part(me_x)
        spread_sources(1, 4)
        others(me_u, N_ROW, source_send)
        k.s_far[me_u] = source_part(me_u)
        others(me_x, N_X, lambda x: far_r(x, x).wait_recv())
        k.r_chunk[...] = total_of(k.r_far, N_X).astype(BF16)
        piece_step(lambda w: sum_r(w, me_q).start())

        others(me_y, N_Y, lambda p: far_a(p, p).wait_recv())
        k.d_part[...] = total_of(k.d_across, N_Y).astype(BF16)
        pair_d.start()

        @pl.when(me_q < PIECES)
        def _():
            k.r_land[me_q] = part(k.r_chunk, me_q)[...]
            others(me_q, N_COL, lambda p: sum_r(me_q, p).wait_recv())
            piece(k.g_all, me_q, here.core, me_x)[...] = total_of(k.r_land, N_COL).astype(BF16)
            others(me_q, N_COL, lambda p: back_r(p, me_q).start())

        others(me_u, N_ROW, lambda u: far_s(u, u).wait_recv())
        share = src[...].astype(F32) - entity_rate * total_of(k.s_far, N_ROW)
        k.src_new[...] = share.astype(BF16)
        src_gather, dst_gather = gathers[1]
        if again:
            src_gather.start()

        others(me_y, N_Y, lambda p: far_o(p, p).wait_recv())
        pair_d.wait_recv()
        share = total_of(k.d_own, N_Y) + k.d_last[...].astype(F32)
        k.dst_new[...] = (dst[...].astype(F32) - entity_rate * share).astype(BF16)
        if again:
            dst_gather.start()

        piece_step(lambda w: back_r(w, w).wait_recv())
        others(me_x, N_X, lambda p: wide_r(p, me_x).start())
        last_r(here.core, me_x).start()
        if again:
            for swap in swaps:
                swap.wait()
            read_lists(1, *lists_away)
            dst_gather.forward()
        others(me_x, N_X, relation_forward)
        if again:
            src_gather.forward()
        every(N_X, lambda x: last_r(1 - here.core, x).wait_recv())
        for start in range(0, rels, CHUNK):
            at = pl.ds(start, min(CHUNK, rels - start))
            grads = k.g_all[pl.ds(0, width), at].astype(F32)
            history = k.his[:, at] + grads * grads
            k.his[:, at] = history
            k.rel[:, at] = k.rel[:, at] - relation_rate * grads / jnp.sqrt(history)

        every(N_X, lambda x: near_r(x).wait_send())
        others(me_x, N_X, lambda x: far_r(x, me_x).wait_send())
        piece_step(lambda w: sum_r(w, me_q).wait_send())

        @pl.when(me_q < PIECES)
        def _():
            others(me_q, N_COL, lambda p: back_r(p, me_q).wait_send())

        others(me_x, N_X, lambda p: wide_r(p, me_x).wait_send())
        every(N_X, lambda x: last_r(here.core, x).wait_send())
        every(N_ROW, lambda u: near_s(u).wait_send())
        others(me_u, N_ROW, lambda u: far_s(u, me_u).wait_send())
        others(me_y, N_Y, lambda p: far_a(p, me_y).wait_send())
        others(me_y, N_Y, lambda p: far_o(p, me_y).wait_send())
        pair_d.wait_send()


    read_lists(0, *lists_here)
    for load in loads:
        load.wait()
    cast_relations()
    pick_relations()
    dst_gather.forward()
    src_gather.forward()
    src_gather.arrive()
    pick_sources()
    score(dst_gather)
    src_gather.drain()
    dst_gather.drain()
    reduce(k.src, k.dst, True)
    src_gather, dst_gather = gathers[1]
    cast_relations()
    pick_relations()
    src_gather.arrive()
    pick_sources()
    score(dst_gather)
    src_gather.drain()
    dst_gather.drain()
    reduce(k.src_new, k.dst_new, False)


def on_device(
    source_table, dest_table, relations, rel_history, src_ids, rel_ids, dst_ids, neg_ids, counts
):
    src, dst = source_table[0].T, dest_table[0].T
    rel, history = relations.T, rel_history.T
    blocks, negs = neg_ids.shape[3:]
    count = jnp.broadcast_to(counts[0, 0][:, None], (2, TILE))
    lists = [src_ids[0, 0], rel_ids[0, 0], dst_ids[0, 0], neg_ids[0, 0].reshape(2 * blocks, negs), count]
    vm, far = pl.BlockSpec(memory_space=pltpu.VMEM), pl.BlockSpec(memory_space=pl.ANY)
    sem = pltpu.SemaphoreType.DMA
    src, dst, rel, history = pl.pallas_call(
        kernel,
        out_shape=[jax.ShapeDtypeStruct(a.shape, a.dtype) for a in (src, dst, rel, history)],
        in_specs=[vm] * 7 + [far] * 2,
        out_specs=[vm] * 4,
        scratch_shapes=[pltpu.VMEM(a.shape, a.dtype) for a in lists]
        + [make(src.shape[0]) for make in SCRATCH.values()]
        + [sem((n,)) for n in SEMS.values() for _ in range(2)]
        + [sem((2,))],
        compiler_params=pltpu.CompilerParams(
            collective_id=0, has_side_effects=True, vmem_limit_bytes=VMEM_BYTES
        ),
    )(src, dst, *lists, rel, history)
    return (src.T[None], dst.T[None], rel.T, history.T)


def solution(mesh):
    placed = (
        P("row", "col", None),
        P("col", "row", None),
        P(),
        P(),
        P("row", "col", None, None),
        P("row", "col", None, None),
        P("row", "col", None, None),
        P("row", "col", None, None, None),
        P("row", "col", None),
    )
    return jax.shard_map(
        on_device,
        mesh=mesh,
        in_specs=placed,
        out_specs=(P("row", "col", None), P("col", "row", None), P(), P()),
        check_vma=False,
    )
```

time: 1740 us -> 238 us (0.14)
  waiting for transfers between devices: 1060 us -> 0 us
  starting transfers between devices: 233 us -> 0 us
  Pallas kernels: 0 us -> 224 us
  other arithmetic: 189 us -> 0 us
  local copies, waits for them, and re-layouts: 196 us -> 10.5 us
  matrix products: 27.2 us -> 0 us
    psum x2 -> x0, waiting for transfers between devices: 382 us -> none  [relation_step(): total = lax.psum(grads, ('row', 'col'))]
    unnamed x12 -> x0, waiting for transfers between devices: 331 us -> none
    ppermute x2 -> x0, starting transfers between devices: 233 us -> none  [swapped(): lax.ppermute(shard, axis, [(i, i ^ 1 << bit) for i in range(lax.axis_size...]
    pallas_call x0 -> x1, Pallas kernels: none -> 224 us  [on_device(): pl.pallas_call(kernel, out_shape=[jax.ShapeDtypeStruct(a.shape, a.dtype)...]
    all_gather x4 -> x0, waiting for transfers between devices: 167 us -> none  [the longest x1 50.5 us: on_device(): partner_block = lax.all_gather(partner_share, 'row', axis=0, tiled=True)]
    reduce_scatter x2 -> x0, waiting for transfers between devices: 147 us -> none  [the longest x1 73.5 us: on_device(): lax.psum_scatter(moved.astype(jnp.float32).astype(jnp.bfloat16), 'row', s...]
    scatter-add x12 -> x0, other arithmetic: 135 us -> none  [the longest x3 34.5 us: block_terms(): grad_dst = grad_dst.at[neg_pick].add(grad_negrows)]
    gather x18 -> x0, local copies, waits for them, and re-layouts: 80.3 us -> none  [the longest x6 22.2 us: block_terms(): source = src_block[src_pick].astype(jnp.float32)]
  transfers between devices with their start and end apart: 12 -> 0, of which waited for: 12 -> 0; matrix products, arithmetic and copies ran while one was open for 3% -> 0% of each run, Pallas kernels for 0% -> 0%
where the time goes in v3:
time: 238 us; the launch traced here: 235 us
  Pallas kernels  224 us (94%)
  local copies, waits for them, and re-layouts  10.5 us (4%)
    pallas_call x1, Pallas kernels, on_device(): pl.pallas_call(kernel, out_shape=[jax.ShapeDtypeStruct(a.shape, a.dtype)...  224 us
    unnamed x6, local copies, waits for them, and re-layouts  7.84 us

profile of v3, /device:TPU:25, one launch (start us, length us, event | category | flops | bytes accessed | tf_op | source)
XLA Modules:
  0.0 234.8 jit_solution(1430028525515846928)
XLA Ops:
  0.6 1.3 broadcast_in_dim.14.refs_6_
  1.9 1.4 reshape_squeeze.3.refs_5_
  3.3 223.6 %shard_map.120 = (bf16[400,128]{1,0:T(8,128)(2,1)}, bf16[400,256]{1,0:T(8,128)(2,1)}, f32[400,1345]{1,0:T(8,128)}, f32[400,1345]{1,0:T(8,128)}) custom-call(bf16[400,128]{1,0:T(8,128)(2,1)} %bitcast.26, bf16[400,256]{1,0:T(8,128)(2,1)} %bitcast.25, s32[2,4000]{1,0:T(2,128)} %bitcast.28, s32[2,4000]{1,0:T(2,128)} %bitcast.29, s32[2,4000]{1,0:T(2,128)} %bitcast.30, ...), custom_call_target="tpu_custom_call" | custom-call | tf_op jit(solution)/shard_map/pallas_call | solution.py:565
  227.0 1.5 copy.17
  228.5 1.6 copy.18
  230.1 0.0 copy-start
  230.1 3.3 %copy.19 = f32[1345,400]{0,1:T(8,128)} copy(f32[1345,400]{0,1:T(8,128)} %bitcast.23) | data formatting | bytes 4304000
  233.4 0.0 copy-done
  233.4 1.4 copy.20
Async XLA Ops:
  230.1 3.3 %copy-start = (f32[400,1345]{1,0:T(8,128)S(1)}, f32[400,1345]{1,0:T(8,128)}, u32[]{:S(2)}) copy-start(f32[400,1345]{1,0:T(8,128)} %get-tuple-element.11) | copy-start | bytes 6456004

commit v4 on v3

--- a/solution.py
+++ b/solution.py
@@ -11,15 +11,16 @@
 NT = (((1,), (1,)), ((), ()))
 entity_rate = 0.3
 relation_rate = 0.5
-N_X, N_Y = 4, 4
+N_Y = 4
 N_ROW, N_COL = 8, 16
 HALF_COL = 8
 TILE, LIVE = 512, 500
 TILES = 8
 CHUNK, PAIR = 256, 512
 SLOTS = TILES * TILE
+UNROLL = 4
 REL_HALF, REL_CUT, REL_PIECE = 208, 384, 16
-REL_ROWS, REL_WIDE = 2 * REL_HALF, N_X * REL_CUT
+REL_ROWS, REL_WIDE = 2 * REL_HALF, N_Y * REL_CUT
 PIECES = REL_HALF // REL_PIECE
 VMEM_BYTES = 60 * 2**20
 
@@ -31,14 +32,11 @@
         self.x, self.y = lax.div(self.col, 4), lax.div(self.row, 2)
         self.z_hi = lax.rem(self.row, 2)
         self.xz = lax.div(self.col, 2)
-        self.yz = self.row * 2 + lax.rem(self.xz, 2)
+        self.plane = self.x * 4 + self.z_hi * 2 + lax.rem(self.xz, 2)
 
     def sibling(self, p=None):
         return {"row": self.row, "col": self.col + 1 - 2 * self.core}
 
-    def at_x(self, p):
-        return {"row": self.row, "col": 4 * p + lax.rem(self.col, 4)}
-
     def at_xz(self, p):
         return {"row": self.row, "col": 2 * p + self.core}
 
@@ -48,8 +46,9 @@
     def across(self, p=None):
         return {"row": self.row + 1 - 2 * self.z_hi, "col": self.col}
 
-    def at_yz(self, p):
-        return {"row": lax.div(p, 2), "col": 4 * self.x + 2 * lax.rem(p, 2) + self.core}
+    def at_plane(self, p):
+        x, z = lax.div(p, 4), lax.rem(p, 4)
+        return {"row": 2 * self.y + lax.div(z, 2), "col": 4 * x + 2 * lax.rem(z, 2) + self.core}
 
     def partner(self, p=None):
         return {"row": self.row, "col": lax.rem(self.col + HALF_COL, N_COL)}
@@ -191,14 +190,13 @@
     gr_all=lambda w: pltpu.VMEM((w, SLOTS), BF16),
     g=lambda w: pltpu.VMEM((w, SLOTS), F32),
     mm=lambda w: pltpu.VMEM((PAIR, SLOTS), BF16),
-    cnt=lambda w: pltpu.VMEM((TILES // 2, 2048, 128), F32),
     ohs=lambda w: pltpu.VMEM((2048, TILE), BF16),
     ohr=lambda w: pltpu.VMEM((REL_WIDE, TILE), BF16),
+    cnt=lambda w: pltpu.VMEM((TILES // 2, 2048, 128), F32),
     lists=lambda w: pltpu.VMEM((8, SLOTS), jnp.int32),
     gd=lambda w: pltpu.VMEM((w, 2048), BF16),
     gs=lambda w: pltpu.VMEM((w, 2048), BF16),
     gr=lambda w: pltpu.VMEM((REL_ROWS, REL_WIDE), BF16),
-    g_all=lambda w: pltpu.VMEM((REL_ROWS, REL_WIDE), BF16),
     s_near=lambda w: pltpu.VMEM((N_ROW, w, 128), BF16),
     s_part=lambda w: pltpu.VMEM((N_ROW, w, 128), BF16),
     s_far=lambda w: pltpu.VMEM((N_ROW, w, 128), BF16),
@@ -206,14 +204,14 @@
     d_own=lambda w: pltpu.VMEM((N_Y, w, 256), BF16),
     d_part=lambda w: pltpu.VMEM((w, 256), BF16),
     d_last=lambda w: pltpu.VMEM((w, 256), BF16),
-    r_near=lambda w: pltpu.VMEM((N_X, REL_HALF, REL_CUT), BF16),
-    r_part=lambda w: pltpu.VMEM((N_X, REL_HALF, REL_CUT), BF16),
-    r_far=lambda w: pltpu.VMEM((N_X, REL_HALF, REL_CUT), BF16),
+    r_near=lambda w: pltpu.VMEM((N_Y, REL_HALF, REL_CUT), BF16),
+    r_part=lambda w: pltpu.VMEM((N_Y, REL_HALF, REL_CUT), BF16),
+    r_far=lambda w: pltpu.VMEM((N_Y, REL_HALF, REL_CUT), BF16),
     r_chunk=lambda w: pltpu.VMEM((REL_HALF, REL_CUT), BF16),
     r_land=lambda w: pltpu.VMEM((N_COL, REL_PIECE, REL_CUT), BF16),
 )
 SEMS = dict(
-    swap=5, near_r=N_X, far_r=N_X, sum_r=N_COL, back_r=N_COL, wide_r=N_X, last_r=N_X, near_s=N_ROW, far_s=N_ROW,
+    swap=5, near_r=N_Y, far_r=N_Y, sum_r=N_COL, back_r=N_COL, wide_r=N_Y, last_r=N_Y, near_s=N_ROW, far_s=N_ROW,
     far_a=N_Y, far_o=N_Y, pair_d=1, src_far=N_ROW, src_near=N_ROW, dst_pair=1, dst_first=N_Y, dst_second=N_Y,
 )
 
@@ -229,8 +227,9 @@
         setattr(k, name, refs.pop(0))
     lists_here = [refs.pop(0) for _ in range(5)]
     rel_in, his_in = refs.pop(0), refs.pop(0)
-    for name in ("src_new", "dst_new", "rel", "his"):
+    for name in ("src_new", "dst_new", "g_0", "g_1"):
         setattr(k, name, refs.pop(0))
+    k.rel, k.his = refs.pop(0), refs.pop(0)
     lists_away = [refs.pop(0) for _ in range(5)]
     for name in SCRATCH:
         setattr(k, name, refs.pop(0))
@@ -240,12 +239,12 @@
     half = width // 2
     rels = rel_in.shape[1]
     here = Place()
-    me_x, me_y, me_u, me_q = here.x, here.y, here.xz, here.yz
+    me_y, me_u, me_q = here.y, here.xz, here.plane
 
     loads = [pltpu.make_async_copy(a, b, load_sems.at[i]) for i, (a, b) in enumerate([(rel_in, k.rel), (his_in, k.his)])]
     for load in loads:
         load.start()
-    meet(here, [(here.core, 2, here.sibling), (me_u, N_ROW, here.at_xz), (me_q, N_COL, here.at_yz)])
+    meet(here, [(here.core, 2, here.sibling), (me_y, N_Y, here.at_y), (me_q, N_COL, here.at_plane)])
     gathers = []
     for src, dst in ((k.src, k.dst), (k.src_new, k.dst_new)):
         gathers.append((
@@ -276,12 +275,12 @@
     def same(ref, name, peer, slot, device):
         return send(ref, ref, sems[name], peer, slot, device)
 
-    near_r = lambda x: send(rel_cut(k.gr, 1 - here.core, x), k.r_near.at[x], sems["near_r"], x, x, here.sibling())
-    far_r = lambda x, slot: send(k.r_part.at[x], k.r_far.at[slot], sems["far_r"], x, slot, here.at_x(x))
-    sum_r = lambda w, slot: send(part(k.r_chunk, w), k.r_land.at[slot], sems["sum_r"], w, slot, here.at_yz(w))
-    back_r = lambda p, w: same(piece(k.g_all, w, here.core, me_x), "back_r", p, w, here.at_yz(p))
-    wide_r = lambda p, x: same(rel_cut(k.g_all, here.core, x), "wide_r", p, x, here.at_x(p))
-    last_r = lambda core, x: same(rel_cut(k.g_all, core, x), "last_r", x, x, here.sibling())
+    near_r = lambda y: send(rel_cut(k.gr, 1 - here.core, y), k.r_near.at[y], sems["near_r"], y, y, here.sibling())
+    far_r = lambda y, slot: send(k.r_part.at[y], k.r_far.at[slot], sems["far_r"], y, slot, here.at_y(y))
+    sum_r = lambda w, slot: send(part(k.r_chunk, w), k.r_land.at[slot], sems["sum_r"], w, slot, here.at_plane(w))
+    back_r = lambda g, p, w: same(piece(g, w, here.core, me_y), "back_r", p, w, here.at_plane(p))
+    wide_r = lambda g, p, y: same(rel_cut(g, here.core, y), "wide_r", p, y, here.at_y(p))
+    last_r = lambda g, core, y: same(rel_cut(g, core, y), "last_r", y, y, here.sibling())
     near_s = lambda u: send(gs_cut(2 * u + 1 - here.core), k.s_near.at[u], sems["near_s"], u, u, here.sibling())
     far_s = lambda u, slot: send(k.s_part.at[u], k.s_far.at[slot], sems["far_s"], u, slot, here.at_xz(u))
     far_a = lambda p, slot: send(
@@ -301,7 +300,7 @@
 
     def read_lists(turn, sid, rid, did, nid, count):
         k.lists[...] = jnp.full(k.lists.shape, -1, jnp.int32)
-        limit = count[pl.ds(turn, 1), pl.ds(0, LIVE)]
+        limit = jnp.broadcast_to(count[:, pl.ds(turn, 1)], (1, LIVE))
         lane = lax.broadcasted_iota(jnp.int32, (1, LIVE), 1)
         for t in range(TILES):
             own, to = pl.ds(t * LIVE, LIVE), pl.ds(t * TILE, LIVE)
@@ -310,7 +309,7 @@
             k.lists[pl.ds(2, 1), to] = jnp.where(lane + t * LIVE < limit, did[pl.ds(turn, 1), own], -1)
         blocks = TILES // 2
         for b in range(blocks):
-            ids = nid[pl.ds(turn * blocks + b, 1), :]
+            ids = nid[turn, pl.ds(b, 1), :]
             low = onehot(128, 0, ids & 127)
             high = onehot(16, 0, ids >> 7)
             total = lax.dot_general(low, high, NT, preferred_element_type=F32) * (1.0 / (2 * LIVE))
@@ -362,23 +361,25 @@
                 turned = lax.dot_general(eye, some, NT, preferred_element_type=F32)
                 k.dnat[pl.ds(h * CHUNK, CHUNK), :] = turned.astype(BF16)
 
-            def step(t):
-                did = k.lists[pl.ds(2, 1), tile_at(t)]
-                rot = k.rot[:, tile_at(t)]
-                for h in range(2):
-                    down = pl.ds(h * CHUNK, CHUNK)
-                    base = y * PAIR + h * CHUNK
-                    lean = jnp.tanh(jnp.dot(k.dnat[down, :], rot, preferred_element_type=F32))
-                    share = k.cnt[lax.div(t, 2), pl.ds(pl.multiple_of(base, CHUNK), CHUNK), :]
-                    share = jnp.concatenate([share] * (TILE // 128), 1)
-                    hit = lax.broadcasted_iota(jnp.int32, (CHUNK, TILE), 0) + base == did
-                    slope = jnp.where(hit, share + 1, share)
-                    k.mm[down, tile_at(t)] = (slope * lean + jnp.where(hit, share - 1, share)).astype(BF16)
-                k.g[:, tile_at(t)] += jnp.dot(
-                    k.dst_all[:, tile_at(y, PAIR)], k.mm[:, tile_at(t)], preferred_element_type=F32
-                )
-
-            every(TILES, step)
+            def leans(t, h):
+                down = pl.ds(h * CHUNK, CHUNK)
+                base = y * PAIR + h * CHUNK
+                lean = jnp.tanh(jnp.dot(k.dnat[down, :], k.rot[:, tile_at(t)], preferred_element_type=F32))
+                share = k.cnt[lax.div(t, 2), pl.ds(pl.multiple_of(base, CHUNK), CHUNK), :]
+                wide = lambda a: jnp.concatenate([a] * (TILE // 128), 1)
+                hit = lax.broadcasted_iota(jnp.int32, (CHUNK, TILE), 0) == k.lists[pl.ds(2, 1), tile_at(t)] - base
+                slope = jnp.where(hit, wide(share + 1), wide(share))
+                k.mm[down, tile_at(t)] = (slope * lean + jnp.where(hit, wide(share - 1), wide(share))).astype(BF16)
+
+            def step(u):
+                for i in range(UNROLL):
+                    for h in range(2):
+                        leans(u * UNROLL + i, h)
+                for i in range(UNROLL):
+                    at = tile_at(u * UNROLL + i)
+                    k.g[:, at] += jnp.dot(k.dst_all[:, tile_at(y, PAIR)], k.mm[:, at], preferred_element_type=F32)
+
+            every(TILES // UNROLL, step)
             total = lax.dot_general(k.rot[...], k.mm[...], NT, preferred_element_type=F32)
             k.gd[:, tile_at(y, PAIR)] = total.astype(BF16)
 
@@ -404,9 +405,10 @@
         every(TILES, step)
 
     def spread(grads, row, base):
+        hot = k.mm
         for t in range(TILES):
-            k.mm[:, pl.ds(t * TILE, TILE)] = onehot(PAIR, base, k.lists[pl.ds(row, 1), pl.ds(t * TILE, TILE)])
-        return lax.dot_general(grads[...], k.mm[...], NT, preferred_element_type=F32).astype(BF16)
+            hot[:, pl.ds(t * TILE, TILE)] = onehot(PAIR, base, k.lists[pl.ds(row, 1), pl.ds(t * TILE, TILE)])
+        return lax.dot_general(grads[...], hot[...], NT, preferred_element_type=F32).astype(BF16)
 
     def spread_relations():
         k.gr[pl.ds(width, REL_ROWS - width), :] = jnp.zeros((REL_ROWS - width, REL_WIDE), BF16)
@@ -425,102 +427,116 @@
 
         every(REL_WIDE // PAIR, step)
 
-    def spread_sources(first, last):
+    def spread_sources():
         def step(c):
             k.gs[:, tile_at(c, PAIR)] = spread(k.rot, 0, c * PAIR)
             near_s(2 * c).start()
             near_s(2 * c + 1).start()
-            return 0
-
-        lax.fori_loop(first, last, lambda c, _: step(c), 0)
-
-    def relation_part(x):
-        near_r(x).wait_recv()
-        return (rel_cut(k.gr, here.core, x)[...].astype(F32) + k.r_near[x].astype(F32)).astype(BF16)
-
-    def relation_send(x):
-        k.r_part[x] = relation_part(x)
-        far_r(x, me_x).start()
-
-    def source_part(u):
+
+            @pl.when(c == 0)
+            def _():
+                others(me_y, N_Y, relation_send)
+                k.r_far[me_y] = relation_part(me_y)
+
+            @pl.when(c > 0)
+            def _():
+                source_send(2 * c - 2)
+                source_send(2 * c - 1)
+
+            @pl.when(c == 2)
+            def _():
+                others(me_y, N_Y, lambda p: far_a(p, p).wait_recv())
+                k.d_part[...] = total_of(k.d_across, N_Y).astype(BF16)
+                pair_d.start()
+
+        every(2048 // PAIR, step)
+        source_send(N_ROW - 2)
+        source_send(N_ROW - 1)
+
+    def relation_part(y):
+        near_r(y).wait_recv()
+        return (rel_cut(k.gr, here.core, y)[...].astype(F32) + k.r_near[y].astype(F32)).astype(BF16)
+
+    def relation_send(y):
+        k.r_part[y] = relation_part(y)
+        far_r(y, me_y).start()
+
+    def source_send(u):
         near_s(u).wait_recv()
-        return (gs_cut(2 * u + here.core)[...].astype(F32) + k.s_near[u].astype(F32)).astype(BF16)
-
-    def source_send(u):
-        k.s_part[u] = source_part(u)
-        far_s(u, me_u).start()
-
-    def relation_forward(x):
-        wide_r(x, x).wait_recv()
-        last_r(here.core, x).start()
-
-    def reduce(src, dst, again):
+        both = (gs_cut(2 * u + here.core)[...].astype(F32) + k.s_near[u].astype(F32)).astype(BF16)
+
+        @pl.when(u == me_u)
+        def _():
+            k.s_far[u] = both
+
+        @pl.when(u != me_u)
+        def _():
+            k.s_part[u] = both
+            far_s(u, me_u).start()
+
+    def reduce(src, dst, g_all, again):
+        src_gather, dst_gather = gathers[1]
         edge_grads()
         spread_relations()
-        spread_sources(0, 1)
-        others(me_x, N_X, relation_send)
-        k.r_far[me_x] = relation_part(me_x)
-        spread_sources(1, 4)
-        others(me_u, N_ROW, source_send)
-        k.s_far[me_u] = source_part(me_u)
-        others(me_x, N_X, lambda x: far_r(x, x).wait_recv())
-        k.r_chunk[...] = total_of(k.r_far, N_X).astype(BF16)
+        spread_sources()
+        others(me_y, N_Y, lambda y: far_r(y, y).wait_recv())
+        k.r_chunk[...] = total_of(k.r_far, N_Y).astype(BF16)
         piece_step(lambda w: sum_r(w, me_q).start())
 
-        others(me_y, N_Y, lambda p: far_a(p, p).wait_recv())
-        k.d_part[...] = total_of(k.d_across, N_Y).astype(BF16)
-        pair_d.start()
+        others(me_y, N_Y, lambda p: far_o(p, p).wait_recv())
+        own = total_of(k.d_own, N_Y)
 
         @pl.when(me_q < PIECES)
         def _():
             k.r_land[me_q] = part(k.r_chunk, me_q)[...]
             others(me_q, N_COL, lambda p: sum_r(me_q, p).wait_recv())
-            piece(k.g_all, me_q, here.core, me_x)[...] = total_of(k.r_land, N_COL).astype(BF16)
-            others(me_q, N_COL, lambda p: back_r(p, me_q).start())
+            piece(g_all, me_q, here.core, me_y)[...] = total_of(k.r_land, N_COL).astype(BF16)
+            others(me_q, N_COL, lambda p: back_r(g_all, p, me_q).start())
 
         others(me_u, N_ROW, lambda u: far_s(u, u).wait_recv())
         share = src[...].astype(F32) - entity_rate * total_of(k.s_far, N_ROW)
         k.src_new[...] = share.astype(BF16)
-        src_gather, dst_gather = gathers[1]
         if again:
             src_gather.start()
 
-        others(me_y, N_Y, lambda p: far_o(p, p).wait_recv())
         pair_d.wait_recv()
-        share = total_of(k.d_own, N_Y) + k.d_last[...].astype(F32)
+        share = own + k.d_last[...].astype(F32)
         k.dst_new[...] = (dst[...].astype(F32) - entity_rate * share).astype(BF16)
+
+        piece_step(lambda w: back_r(g_all, w, w).wait_recv())
+        others(me_y, N_Y, lambda p: wide_r(g_all, p, me_y).start())
+        last_r(g_all, here.core, me_y).start()
         if again:
             dst_gather.start()
-
-        piece_step(lambda w: back_r(w, w).wait_recv())
-        others(me_x, N_X, lambda p: wide_r(p, me_x).start())
-        last_r(here.core, me_x).start()
-        if again:
             for swap in swaps:
                 swap.wait()
             read_lists(1, *lists_away)
-            dst_gather.forward()
-        others(me_x, N_X, relation_forward)
+
+        def relation_forward(y):
+            wide_r(g_all, y, y).wait_recv()
+            last_r(g_all, here.core, y).start()
+
+        others(me_y, N_Y, relation_forward)
         if again:
             src_gather.forward()
-        every(N_X, lambda x: last_r(1 - here.core, x).wait_recv())
-        for start in range(0, rels, CHUNK):
-            at = pl.ds(start, min(CHUNK, rels - start))
-            grads = k.g_all[pl.ds(0, width), at].astype(F32)
-            history = k.his[:, at] + grads * grads
-            k.his[:, at] = history
-            k.rel[:, at] = k.rel[:, at] - relation_rate * grads / jnp.sqrt(history)
-
-        every(N_X, lambda x: near_r(x).wait_send())
-        others(me_x, N_X, lambda x: far_r(x, me_x).wait_send())
+            dst_gather.forward()
+        every(N_Y, lambda y: last_r(g_all, 1 - here.core, y).wait_recv())
+        if again:
+            for start in range(0, rels, CHUNK):
+                at = pl.ds(start, min(CHUNK, rels - start))
+                grads = g_all[pl.ds(0, width), at].astype(F32)
+                k.rel[:, at] -= relation_rate * grads / jnp.sqrt(k.his[:, at] + grads * grads)
+
+        every(N_Y, lambda y: near_r(y).wait_send())
+        others(me_y, N_Y, lambda y: far_r(y, me_y).wait_send())
         piece_step(lambda w: sum_r(w, me_q).wait_send())
 
         @pl.when(me_q < PIECES)
         def _():
-            others(me_q, N_COL, lambda p: back_r(p, me_q).wait_send())
-
-        others(me_x, N_X, lambda p: wide_r(p, me_x).wait_send())
-        every(N_X, lambda x: last_r(here.core, x).wait_send())
+            others(me_q, N_COL, lambda p: back_r(g_all, p, me_q).wait_send())
+
+        others(me_y, N_Y, lambda p: wide_r(g_all, p, me_y).wait_send())
+        every(N_Y, lambda y: last_r(g_all, here.core, y).wait_send())
         every(N_ROW, lambda u: near_s(u).wait_send())
         others(me_u, N_ROW, lambda u: far_s(u, me_u).wait_send())
         others(me_y, N_Y, lambda p: far_a(p, me_y).wait_send())
@@ -540,7 +556,7 @@
     score(dst_gather)
     src_gather.drain()
     dst_gather.drain()
-    reduce(k.src, k.dst, True)
+    reduce(k.src, k.dst, k.g_0, True)
     src_gather, dst_gather = gathers[1]
     cast_relations()
     pick_relations()
@@ -549,7 +565,7 @@
     score(dst_gather)
     src_gather.drain()
     dst_gather.drain()
-    reduce(k.src_new, k.dst_new, False)
+    reduce(k.src_new, k.dst_new, k.g_1, False)
 
 
 def on_device(
@@ -557,17 +573,16 @@
 ):
     src, dst = source_table[0].T, dest_table[0].T
     rel, history = relations.T, rel_history.T
-    blocks, negs = neg_ids.shape[3:]
-    count = jnp.broadcast_to(counts[0, 0][:, None], (2, TILE))
-    lists = [src_ids[0, 0], rel_ids[0, 0], dst_ids[0, 0], neg_ids[0, 0].reshape(2 * blocks, negs), count]
+    lists = [src_ids[0, 0], rel_ids[0, 0], dst_ids[0, 0], neg_ids[0, 0], counts[0]]
     vm, far = pl.BlockSpec(memory_space=pltpu.VMEM), pl.BlockSpec(memory_space=pl.ANY)
     sem = pltpu.SemaphoreType.DMA
-    src, dst, rel, history = pl.pallas_call(
+    grads = jax.ShapeDtypeStruct((REL_ROWS, REL_WIDE), BF16)
+    src, dst, *rounds = pl.pallas_call(
         kernel,
-        out_shape=[jax.ShapeDtypeStruct(a.shape, a.dtype) for a in (src, dst, rel, history)],
+        out_shape=[jax.ShapeDtypeStruct(a.shape, a.dtype) for a in (src, dst)] + [grads] * 2,
         in_specs=[vm] * 7 + [far] * 2,
         out_specs=[vm] * 4,
-        scratch_shapes=[pltpu.VMEM(a.shape, a.dtype) for a in lists]
+        scratch_shapes=[pltpu.VMEM(a.shape, a.dtype) for a in [rel, history] + lists]
         + [make(src.shape[0]) for make in SCRATCH.values()]
         + [sem((n,)) for n in SEMS.values() for _ in range(2)]
         + [sem((2,))],
@@ -575,6 +590,10 @@
             collective_id=0, has_side_effects=True, vmem_limit_bytes=VMEM_BYTES
         ),
     )(src, dst, *lists, rel, history)
+    for grads in rounds:
+        grads = grads[: rel.shape[0], : rel.shape[1]].astype(F32)
+        history = history + grads * grads
+        rel = rel - relation_rate * grads / jnp.sqrt(history)
     return (src.T[None], dst.T[None], rel.T, history.T)
 
 

time: 238 us -> 224 us (0.941)
  local copies, waits for them, and re-layouts: 10.5 us -> 1.33 us
  Pallas kernels: 224 us -> 215 us
  other arithmetic: 0 us -> 5.48 us
    pallas_call x1, Pallas kernels: 224 us -> 215 us  [on_device(): pl.pallas_call(kernel, out_shape=[jax.ShapeDtypeStruct(a.shape, a.dtype)...]
    unnamed x6 -> x8, local copies, waits for them, and re-layouts: 7.84 us -> 1.33 us
    transpose x0 -> x1, other arithmetic: none -> 5.48 us  [on_device(): return (src.T[None], dst.T[None], rel.T, history.T)]
where the time goes in v4:
time: 224 us; the launch traced here: 222 us
  Pallas kernels  215 us (96%)
  other arithmetic  5.48 us (2%)
    pallas_call x1, Pallas kernels, on_device(): pl.pallas_call(kernel, out_shape=[jax.ShapeDtypeStruct(a.shape, a.dtype)...  215 us
    transpose x1, other arithmetic, on_device(): return (src.T[None], dst.T[None], rel.T, history.T)  5.48 us

profile of v4, /device:TPU:25, one launch (start us, length us, event | category | flops | bytes accessed | tf_op | source)
XLA Modules:
  0.0 222.1 jit_solution(3607403741612476208)
XLA Ops:
  0.6 0.0 copy-start
  0.6 214.6 %shard_map.120 = (bf16[400,128]{1,0:T(8,128)(2,1)}, bf16[400,256]{1,0:T(8,128)(2,1)}, bf16[416,1536]{1,0:T(8,128)(2,1)}, bf16[416,1536]{1,0:T(8,128)(2,1)}) custom-call(bf16[400,128]{1,0:T(8,128)(2,1)} %bitcast.31, bf16[400,256]{1,0:T(8,128)(2,1)} %bitcast.29, s32[2,4000]{1,0:T(2,128)} %bitcast.32, s32[2,4000]{1,0:T(2,128)} %bitcast.33, s32[2,4000]{1,0:T(2,128)} %bitcast.34, ...), custom_call_target="tpu_custom_call" | custom-call | tf_op jit(solution)/shard_map/pallas_call | solution.py:580
  215.2 0.0 copy-done
  215.3 0.0 copy-start.2
  215.3 0.0 copy-start.1
  215.3 5.5 %fusion.7 = (f32[1345,400]{0,1:T(8,128)}, f32[1345,400]{0,1:T(8,128)}) fusion(bf16[416,1536]{1,0:T(8,128)(2,1)} %get-tuple-element.11, bf16[416,1536]{1,0:T(8,128)(2,1)} %get-tuple-element.10, f32[1345,400]{0,1:T(8,128)} %param.12, f32[1345,400]{0,1:T(8,128)S(1)} %copy-done), kind=kLoop, calls=%fused_computation.11 | loop fusion | flops 6456000 | bytes 10760000 | tf_op jit(solution)/shard_map/transpose | solution.py:597
  220.8 0.0 copy-done.2
  220.8 0.6 copy.15
  221.4 0.0 copy-done.1
  221.4 0.7 copy.16
Async XLA Ops:
  0.6 214.6 %copy-start = (f32[1345,400]{0,1:T(8,128)S(1)}, f32[1345,400]{0,1:T(8,128)}, u32[]{:S(2)}) copy-start(f32[1345,400]{0,1:T(8,128)} %param.11) | copy-start | bytes 6456004
  215.3 5.5 %copy-start.2 = (bf16[400,128]{1,0:T(8,128)(2,1)S(1)}, bf16[400,128]{1,0:T(8,128)(2,1)}, u32[]{:S(2)}) copy-start(bf16[400,128]{1,0:T(8,128)(2,1)} %get-tuple-element.8) | copy-start | bytes 307204
  215.3 6.1 %copy-start.1 = (bf16[400,256]{1,0:T(8,128)(2,1)S(1)}, bf16[400,256]{1,0:T(8,128)(2,1)}, u32[]{:S(2)}) copy-start(bf16[400,256]{1,0:T(8,128)(2,1)} %get-tuple-element.9) | copy-start | bytes 614404

commit v5 on v4

--- a/solution.py
+++ b/solution.py
@@ -320,31 +320,41 @@
         k.relt[...] = jnp.zeros_like(k.relt)
         k.relt[:, pl.ds(0, rels)] = k.rel[...].astype(BF16)
 
-    def pick_relations():
+    def alive(t):
+        return jnp.where(k.lists[pl.ds(2, 1), tile_at(t)] >= 0, 0.5, 0.0)
+
+    def both(ref, t):
+        return ref[t, 0].astype(F32), ref[t, 1].astype(F32)
+
+    def turn(t, sre, sim, rre, rim):
+        rot = jnp.concatenate([sre * rre - sim * rim, sre * rim + sim * rre], 0)
+        k.rot[:, tile_at(t)] = (rot * alive(t)).astype(BF16)
+        k.g[:, tile_at(t)] = jnp.zeros((width, TILE), F32)
+
+    def pick_relations(last):
         def step(t):
             k.ohr[...] = onehot(REL_WIDE, 0, k.lists[pl.ds(1, 1), tile_at(t)])
-            r = jnp.dot(k.relt[...], k.ohr[...], preferred_element_type=F32).astype(BF16)
-            k.r_all[t, 0] = r[:half]
-            k.r_all[t, 1] = r[half:]
+            r = jnp.dot(k.relt[...], k.ohr[...], preferred_element_type=F32)
+            k.r_all[t, 0] = r[:half].astype(BF16)
+            k.r_all[t, 1] = r[half:].astype(BF16)
+            if last:
+                turn(t, *both(k.s_all, t), r[:half], r[half:])
 
         every(TILES, step)
 
-    def pick_sources():
-        def step(t):
+    def pick_sources(first, end, last):
+        def step(t, _):
             sid = k.lists[pl.ds(0, 1), tile_at(t)]
-            alive = jnp.where(k.lists[pl.ds(2, 1), tile_at(t)] >= 0, 0.5, 0.0)
             for c in range(2048 // CHUNK):
                 k.ohs[pl.ds(c * CHUNK, CHUNK), :] = onehot(CHUNK, c * CHUNK, sid)
             s = jnp.dot(k.src_all[...], k.ohs[...], preferred_element_type=F32)
-            sre, sim = s[:half], s[half:]
-            rre, rim = k.r_all[t, 0].astype(F32), k.r_all[t, 1].astype(F32)
-            k.s_all[t, 0] = sre.astype(BF16)
-            k.s_all[t, 1] = sim.astype(BF16)
-            rot = jnp.concatenate([sre * rre - sim * rim, sre * rim + sim * rre], 0)
-            k.rot[:, tile_at(t)] = (rot * alive).astype(BF16)
-            k.g[:, tile_at(t)] = jnp.zeros((width, TILE), F32)
-
-        every(TILES, step)
+            k.s_all[t, 0] = s[:half].astype(BF16)
+            k.s_all[t, 1] = s[half:].astype(BF16)
+            if last:
+                turn(t, s[:half], s[half:], *both(k.r_all, t))
+            return 0
+
+        lax.fori_loop(first, end, step, 0)
 
     def score(dst_gather):
         eye = onehot(CHUNK, 0, lax.broadcasted_iota(jnp.int32, (1, CHUNK), 1))
@@ -392,15 +402,21 @@
         k.d_across[me_y] = gd_cut(2 * me_y + 1 - here.z_hi)[...]
         k.d_own[me_y] = gd_cut(2 * me_y + here.z_hi)[...]
 
-    def edge_grads():
+    def relation_grads():
         def step(t):
-            alive = jnp.where(k.lists[pl.ds(2, 1), tile_at(t)] >= 0, 0.5, 0.0)
-            g = k.g[:, tile_at(t)] * alive
+            g = k.g[:, tile_at(t)] * alive(t)
             gre, gim = g[:half], g[half:]
-            sre, sim = k.s_all[t, 0].astype(F32), k.s_all[t, 1].astype(F32)
-            rre, rim = k.r_all[t, 0].astype(F32), k.r_all[t, 1].astype(F32)
+            sre, sim = both(k.s_all, t)
+            k.gr_all[:, tile_at(t)] = jnp.concatenate([gre * sre + gim * sim, gim * sre - gre * sim], 0).astype(BF16)
+
+        every(TILES, step)
+
+    def source_grads():
+        def step(t):
+            g = k.g[:, tile_at(t)] * alive(t)
+            gre, gim = g[:half], g[half:]
+            rre, rim = both(k.r_all, t)
             k.rot[:, tile_at(t)] = jnp.concatenate([gre * rre + gim * rim, gim * rre - gre * rim], 0).astype(BF16)
-            k.gr_all[:, tile_at(t)] = jnp.concatenate([gre * sre + gim * sim, gim * sre - gre * sim], 0).astype(BF16)
 
         every(TILES, step)
 
@@ -433,11 +449,6 @@
             near_s(2 * c).start()
             near_s(2 * c + 1).start()
 
-            @pl.when(c == 0)
-            def _():
-                others(me_y, N_Y, relation_send)
-                k.r_far[me_y] = relation_part(me_y)
-
             @pl.when(c > 0)
             def _():
                 source_send(2 * c - 2)
@@ -476,8 +487,11 @@
 
     def reduce(src, dst, g_all, again):
         src_gather, dst_gather = gathers[1]
-        edge_grads()
+        relation_grads()
         spread_relations()
+        source_grads()
+        others(me_y, N_Y, relation_send)
+        k.r_far[me_y] = relation_part(me_y)
         spread_sources()
         others(me_y, N_Y, lambda y: far_r(y, y).wait_recv())
         k.r_chunk[...] = total_of(k.r_far, N_Y).astype(BF16)
@@ -516,10 +530,14 @@
             wide_r(g_all, y, y).wait_recv()
             last_r(g_all, here.core, y).start()
 
-        others(me_y, N_Y, relation_forward)
         if again:
             src_gather.forward()
             dst_gather.forward()
+            src_gather.arrive()
+            pick_sources(0, TILES // 2, False)
+        others(me_y, N_Y, relation_forward)
+        if again:
+            pick_sources(TILES // 2, TILES, False)
         every(N_Y, lambda y: last_r(g_all, 1 - here.core, y).wait_recv())
         if again:
             for start in range(0, rels, CHUNK):
@@ -548,20 +566,18 @@
     for load in loads:
         load.wait()
     cast_relations()
-    pick_relations()
+    pick_relations(False)
     dst_gather.forward()
     src_gather.forward()
     src_gather.arrive()
-    pick_sources()
+    pick_sources(0, TILES, True)
     score(dst_gather)
     src_gather.drain()
     dst_gather.drain()
     reduce(k.src, k.dst, k.g_0, True)
     src_gather, dst_gather = gathers[1]
     cast_relations()
-    pick_relations()
-    src_gather.arrive()
-    pick_sources()
+    pick_relations(True)
     score(dst_gather)
     src_gather.drain()
     dst_gather.drain()

time: 224 us -> 222 us (level)
  Pallas kernels: 215 us -> 211 us
    pallas_call x1, Pallas kernels: 215 us -> 211 us  [on_device(): pl.pallas_call(kernel, out_shape=[jax.ShapeDtypeStruct(a.shape, a.dtype)...]
where the time goes in v5:
time: 222 us; the launch traced here: 218 us
  Pallas kernels  211 us (95%)
  other arithmetic  5.48 us (2%)
    pallas_call x1, Pallas kernels, on_device(): pl.pallas_call(kernel, out_shape=[jax.ShapeDtypeStruct(a.shape, a.dtype)...  211 us
    transpose x1, other arithmetic, on_device(): return (src.T[None], dst.T[None], rel.T, history.T)  5.48 us

profile of v5, /device:TPU:25, one launch (start us, length us, event | category | flops | bytes accessed | tf_op | source)
XLA Modules:
  0.0 218.5 jit_solution(8629752370427717744)
XLA Ops:
  0.6 0.0 copy-start
  0.6 211.0 %shard_map.120 = (bf16[400,128]{1,0:T(8,128)(2,1)}, bf16[400,256]{1,0:T(8,128)(2,1)}, bf16[416,1536]{1,0:T(8,128)(2,1)}, bf16[416,1536]{1,0:T(8,128)(2,1)}) custom-call(bf16[400,128]{1,0:T(8,128)(2,1)} %bitcast.31, bf16[400,256]{1,0:T(8,128)(2,1)} %bitcast.29, s32[2,4000]{1,0:T(2,128)} %bitcast.32, s32[2,4000]{1,0:T(2,128)} %bitcast.33, s32[2,4000]{1,0:T(2,128)} %bitcast.34, ...), custom_call_target="tpu_custom_call" | custom-call | tf_op jit(solution)/shard_map/pallas_call | solution.py:596
  211.6 0.0 copy-done
  211.6 0.0 copy-start.2
  211.6 0.0 copy-start.1
  211.7 5.5 %fusion.7 = (f32[1345,400]{0,1:T(8,128)}, f32[1345,400]{0,1:T(8,128)}) fusion(bf16[416,1536]{1,0:T(8,128)(2,1)} %get-tuple-element.11, bf16[416,1536]{1,0:T(8,128)(2,1)} %get-tuple-element.10, f32[1345,400]{0,1:T(8,128)} %param.12, f32[1345,400]{0,1:T(8,128)S(1)} %copy-done), kind=kLoop, calls=%fused_computation.11 | loop fusion | flops 6456000 | bytes 10760000 | tf_op jit(solution)/shard_map/transpose | solution.py:613
  217.1 0.0 copy-done.2
  217.1 0.6 copy.15
  217.8 0.0 copy-done.1
  217.8 0.7 copy.16
Async XLA Ops:
  0.6 211.0 %copy-start = (f32[1345,400]{0,1:T(8,128)S(1)}, f32[1345,400]{0,1:T(8,128)}, u32[]{:S(2)}) copy-start(f32[1345,400]{0,1:T(8,128)} %param.11) | copy-start | bytes 6456004
  211.6 5.5 %copy-start.2 = (bf16[400,128]{1,0:T(8,128)(2,1)S(1)}, bf16[400,128]{1,0:T(8,128)(2,1)}, u32[]{:S(2)}) copy-start(bf16[400,128]{1,0:T(8,128)(2,1)} %get-tuple-element.8) | copy-start | bytes 307204
  211.6 6.1 %copy-start.1 = (bf16[400,256]{1,0:T(8,128)(2,1)S(1)}, bf16[400,256]{1,0:T(8,128)(2,1)}, u32[]{:S(2)}) copy-start(bf16[400,256]{1,0:T(8,128)(2,1)} %get-tuple-element.9) | copy-start | bytes 614404

commit v6 on v5

--- a/solution.py
+++ b/solution.py
@@ -11,14 +11,14 @@
 NT = (((1,), (1,)), ((), ()))
 entity_rate = 0.3
 relation_rate = 0.5
-N_Y = 4
+N_X, N_Y = 4, 4
 N_ROW, N_COL = 8, 16
 HALF_COL = 8
 TILE, LIVE = 512, 500
 TILES = 8
 CHUNK, PAIR = 256, 512
 SLOTS = TILES * TILE
-UNROLL = 4
+UNROLL = 8
 REL_HALF, REL_CUT, REL_PIECE = 208, 384, 16
 REL_ROWS, REL_WIDE = 2 * REL_HALF, N_Y * REL_CUT
 PIECES = REL_HALF // REL_PIECE
@@ -96,34 +96,51 @@
     def __init__(self, here, mine, table, sems):
         self.here, self.mine, self.to = here, mine, lanes(table, mine.shape[1])
         self.far, self.near = sems[:2], sems[2:]
+        self.me, self.x, self.z = here.xz, lax.div(here.xz, 2), lax.rem(here.xz, 2)
+        self.mate = self.me + 1 - 2 * self.z
         self.slot = lambda p: self.to(2 * p + here.core)
         self.back = lambda p: self.to(2 * p + 1 - here.core)
 
-    def far_copy(self, source, target, p, slot):
-        return send(source, target, self.far, p, slot, self.here.at_xz(p))
+    def far_copy(self, source, target, index, peer, slot):
+        return send(source, target, self.far, index, slot, self.here.at_xz(peer))
 
     def near_copy(self, source, target, p):
         return send(source, target, self.near, p, p, self.here.sibling())
 
+    def along_x(self, z, act):
+        others(self.x, N_X, lambda x: act(2 * x + z))
+
     def start(self):
-        me = self.here.xz
-        others(me, N_ROW, lambda p: self.far_copy(self.mine, self.slot(me), p, me).start())
+        me, mate = self.me, self.mate
+        self.far_copy(self.mine, self.slot(me), mate, mate, me).start()
+        self.along_x(self.z, lambda p: self.far_copy(self.mine, self.slot(me), p, p, me).start())
         self.near_copy(self.mine, self.slot(me), me).start()
         self.slot(me)[...] = self.mine[...]
 
+    def got(self, p):
+        self.far_copy(self.mine, self.slot(p), p, p, p).wait_recv()
+        self.near_copy(self.slot(p), self.slot(p), p).start()
+
+    def forward_mate(self):
+        mate = self.mate
+        self.far_copy(self.mine, self.slot(mate), mate, mate, mate).wait_recv()
+
+        def step(x):
+            self.far_copy(self.slot(mate), self.slot(mate), 2 * x + 1 - self.z, 2 * x + self.z, mate).start()
+
+        others(self.x, N_X, step)
+        self.near_copy(self.slot(mate), self.slot(mate), mate).start()
+
     def forward(self):
-        def step(p):
-            self.far_copy(self.mine, self.slot(p), p, p).wait_recv()
-            self.near_copy(self.slot(p), self.slot(p), p).start()
-
-        others(self.here.xz, N_ROW, step)
+        self.along_x(self.z, self.got)
+        self.along_x(1 - self.z, self.got)
 
     def arrive(self):
         every(N_ROW, lambda p: self.near_copy(self.mine, self.back(p), p).wait_recv())
 
     def drain(self):
-        me = self.here.xz
-        others(me, N_ROW, lambda p: self.far_copy(self.mine, self.slot(me), p, me).wait_send())
+        me = self.me
+        others(me, N_ROW, lambda p: self.far_copy(self.mine, self.slot(me), p, p, me).wait_send())
         every(N_ROW, lambda p: self.near_copy(self.mine, self.slot(p), p).wait_send())
 
 
@@ -252,8 +269,8 @@
             DestGather(here, dst, k.dst_all, sems["dst_pair"] + sems["dst_first"] + sems["dst_second"]),
         ))
     src_gather, dst_gather = gathers[0]
+    src_gather.start()
     dst_gather.start()
-    src_gather.start()
     swaps = [send(a, b, sems["swap"], i, i, here.partner()) for i, (a, b) in enumerate(zip(lists_here, lists_away))]
     for swap in swaps:
         swap.start()
@@ -331,16 +348,17 @@
         k.rot[:, tile_at(t)] = (rot * alive(t)).astype(BF16)
         k.g[:, tile_at(t)] = jnp.zeros((width, TILE), F32)
 
-    def pick_relations(last):
-        def step(t):
+    def pick_relations(first, end, last):
+        def step(t, _):
             k.ohr[...] = onehot(REL_WIDE, 0, k.lists[pl.ds(1, 1), tile_at(t)])
             r = jnp.dot(k.relt[...], k.ohr[...], preferred_element_type=F32)
             k.r_all[t, 0] = r[:half].astype(BF16)
             k.r_all[t, 1] = r[half:].astype(BF16)
             if last:
                 turn(t, *both(k.s_all, t), r[:half], r[half:])
-
-        every(TILES, step)
+            return 0
+
+        lax.fori_loop(first, end, step, 0)
 
     def pick_sources(first, end, last):
         def step(t, _):
@@ -524,6 +542,7 @@
             dst_gather.start()
             for swap in swaps:
                 swap.wait()
+            src_gather.forward_mate()
             read_lists(1, *lists_away)
 
         def relation_forward(y):
@@ -566,8 +585,10 @@
     for load in loads:
         load.wait()
     cast_relations()
-    pick_relations(False)
+    pick_relations(0, TILES // 4, False)
+    src_gather.forward_mate()
     dst_gather.forward()
+    pick_relations(TILES // 4, TILES, False)
     src_gather.forward()
     src_gather.arrive()
     pick_sources(0, TILES, True)
@@ -577,7 +598,7 @@
     reduce(k.src, k.dst, k.g_0, True)
     src_gather, dst_gather = gathers[1]
     cast_relations()
-    pick_relations(True)
+    pick_relations(0, TILES, True)
     score(dst_gather)
     src_gather.drain()
     dst_gather.drain()

time: 222 us -> 215 us (0.968)
  Pallas kernels: 211 us -> 204 us
    pallas_call x1, Pallas kernels: 211 us -> 204 us  [on_device(): pl.pallas_call(kernel, out_shape=[jax.ShapeDtypeStruct(a.shape, a.dtype)...]
where the time goes in v6:
time: 215 us; the launch traced here: 212 us
  Pallas kernels  204 us (95%)
  other arithmetic  5.48 us (3%)
    pallas_call x1, Pallas kernels, on_device(): pl.pallas_call(kernel, out_shape=[jax.ShapeDtypeStruct(a.shape, a.dtype)...  204 us
    transpose x1, other arithmetic, on_device(): return (src.T[None], dst.T[None], rel.T, history.T)  5.48 us

profile of v6, /device:TPU:25, one launch (start us, length us, event | category | flops | bytes accessed | tf_op | source)
XLA Modules:
  0.0 211.7 jit_solution(16247690335749404910)
XLA Ops:
  0.6 0.0 copy-start
  0.6 204.2 %shard_map.120 = (bf16[400,128]{1,0:T(8,128)(2,1)}, bf16[400,256]{1,0:T(8,128)(2,1)}, bf16[416,1536]{1,0:T(8,128)(2,1)}, bf16[416,1536]{1,0:T(8,128)(2,1)}) custom-call(bf16[400,128]{1,0:T(8,128)(2,1)} %bitcast.31, bf16[400,256]{1,0:T(8,128)(2,1)} %bitcast.29, s32[2,4000]{1,0:T(2,128)} %bitcast.32, s32[2,4000]{1,0:T(2,128)} %bitcast.33, s32[2,4000]{1,0:T(2,128)} %bitcast.34, ...), custom_call_target="tpu_custom_call" | custom-call | tf_op jit(solution)/shard_map/pallas_call | solution.py:617
  204.9 0.0 copy-done
  204.9 0.0 copy-start.2
  204.9 0.0 copy-start.1
  204.9 5.5 %fusion.7 = (f32[1345,400]{0,1:T(8,128)}, f32[1345,400]{0,1:T(8,128)}) fusion(bf16[416,1536]{1,0:T(8,128)(2,1)} %get-tuple-element.11, bf16[416,1536]{1,0:T(8,128)(2,1)} %get-tuple-element.10, f32[1345,400]{0,1:T(8,128)} %param.12, f32[1345,400]{0,1:T(8,128)S(1)} %copy-done), kind=kLoop, calls=%fused_computation.11 | loop fusion | flops 6456000 | bytes 10760000 | tf_op jit(solution)/shard_map/transpose | solution.py:634
  210.4 0.0 copy-done.2
  210.4 0.6 copy.15
  211.0 0.0 copy-done.1
  211.0 0.7 copy.16
Async XLA Ops:
  0.6 204.2 %copy-start = (f32[1345,400]{0,1:T(8,128)S(1)}, f32[1345,400]{0,1:T(8,128)}, u32[]{:S(2)}) copy-start(f32[1345,400]{0,1:T(8,128)} %param.11) | copy-start | bytes 6456004
  204.9 5.5 %copy-start.2 = (bf16[400,128]{1,0:T(8,128)(2,1)S(1)}, bf16[400,128]{1,0:T(8,128)(2,1)}, u32[]{:S(2)}) copy-start(bf16[400,128]{1,0:T(8,128)(2,1)} %get-tuple-element.8) | copy-start | bytes 307204
  204.9 6.1 %copy-start.1 = (bf16[400,256]{1,0:T(8,128)(2,1)S(1)}, bf16[400,256]{1,0:T(8,128)(2,1)}, u32[]{:S(2)}) copy-start(bf16[400,256]{1,0:T(8,128)(2,1)} %get-tuple-element.9) | copy-start | bytes 614404
